TPU v7x, 32 devices: a whole 2x2x4 slice. The times are simulated.
32 devices in a mesh: groups: 2 (over y), depth: 4 (over z), rays: 4 (over x, core).
Axes of the slice: x: 2, y: 2, z: 4, core: 2. Of those that a mesh axis runs over, the one named last changes fastest.
Arguments:
- brick_features: bfloat16 [16, 8, 4, 16384], P(None, ('groups', 'depth'), 'rays'), parts along dimension 1, may hold values from -6 to 6
- entry_cells: int32 [8, 4, 1024], P(('groups', 'depth'), 'rays'), parts along dimension 0, may hold values from 0 to 16368
- sample_counts: int32 [8, 4, 1024], P(('groups', 'depth'), 'rays'), parts along dimension 0, may hold values from 1 to 16, as said below
- brick_rank: int32 [8, 4], P(('groups', 'rays')), parts along dimension 0, may hold values from 0 to 3, each once within a row
- input_layer_weight: bfloat16 [16, 128], replicated, may hold values from -1.5 to 1.5
- second_weight: bfloat16 [128, 33], replicated, may hold values from -0.5 to 0.5
- conv_in: bfloat16 [9, 32, 128], replicated, may hold values from -0.375 to 0.375
- conv_mid: bfloat16 [9, 128, 128], replicated, may hold values from -0.1875 to 0.1875
- conv_out: bfloat16 [9, 128, 128], replicated, may hold values from -0.1875 to 0.1875
Outputs:
- frame: bfloat16 [128, 64, 128], P(('groups', 'depth'), 'rays'), parts along dimension 0
There are 2 independent parts, one for each index of `groups`. A program takes and returns all parts, laid end to end along the dimension named above; an argument that names none is the same for every part. Nothing has to cross between parts.
Inputs may be any that keep to these rules, and one draw needn't show every extreme that they name: `sample_counts`: each brick and strip has a level of at most 16; its rays take 1 to that level samples; some brick and strip reaches 16. `brick_rank`: each row is a permutation of the bricks.
All inputs are finite; a program needn't handle non-finite values.
Results may differ from a plain program's by a relative error of at most 0.015.
Values may be sent and summed in bfloat16 or wider, within the bound.
A program may use at most 64 MiB of HBM per device.

v0:
```python
import math

import jax
import jax.numpy as jnp
from jax import lax
from jax.sharding import PartitionSpec as P

SAMPLES = 16
ROWS_OWN = 16
COLS_DEV = 16


def padded_2(x, sides, width):
    for axis, dim in sides:
        size, length = (lax.axis_size(axis), x.shape[dim])
        up = [(i, (i + 1) % size) for i in range(size - 1)]
        down = [(j, i) for i, j in up]
        last = lax.slice_in_dim(x, length - width, length, axis=dim)
        first = lax.slice_in_dim(x, 0, width, axis=dim)
        before = lax.ppermute(last, axis, up)
        after = lax.ppermute(first, axis, down)
        x = jnp.concatenate([before, x, after], axis=dim)
    return x


def blend_sample_values(field, counts, bricks):
    step_len = 8.0 / (SAMPLES * bricks)
    slot_ids = jnp.arange(SAMPLES, dtype=jnp.int32)
    valid = (slot_ids[:, None] < counts[None, :]).astype(jnp.float32)
    optical = step_len * jax.nn.softplus(field[0]) * valid
    earlier = (slot_ids[:, None] > slot_ids[None, :]).astype(jnp.float32)
    before = jnp.dot(earlier, optical, precision=lax.Precision.HIGHEST)
    weights = jnp.exp(-before) * (1.0 - jnp.exp(-optical))
    colour = jnp.sum(weights[None] * field[1:], axis=1)
    return (colour, jnp.sum(optical, axis=0))


def convolve_valid(padded, weights):
    height = padded.shape[0] - 2
    width = padded.shape[1] - 2
    total = jnp.zeros((height * width, weights.shape[2]), jnp.float32)
    for tap in range(9):
        row_offset_shift, shift_col = divmod(tap, 3)
        window = padded[
            row_offset_shift : row_offset_shift + height, shift_col : shift_col + width
        ].reshape(height * width, -1)
        total = total + jnp.dot(window, weights[tap], preferred_element_type=jnp.float32)
    return total.reshape(height, width, weights.shape[2])


def border_padding(source):
    return padded_2(source, (("depth", 0), ("rays", 1)), 1)


def shards(
    brick_features,
    entry_cells,
    sample_counts,
    brick_rank,
    input_layer_weight,
    second_weight,
    conv_in,
    conv_mid,
    conv_out,
):
    bricks = lax.axis_size("depth")
    feat_count = brick_features.shape[0]
    cell_count = brick_features.shape[3]
    windows = cell_count // SAMPLES
    span = SAMPLES * feat_count
    table = (
        brick_features.reshape(feat_count, windows, SAMPLES)
        .transpose(1, 2, 0)
        .reshape(windows, span)
    )
    entries = entry_cells.reshape(-1)
    counts = sample_counts.reshape(-1)
    ranks = brick_rank.reshape(-1)
    total_rays = entries.shape[0]
    block = math.gcd(total_rays, 512)
    shift_bits = (SAMPLES - 1).bit_length()

    def march_block(operands):
        block_entries, block_counts = operands
        window_ids = block_entries // SAMPLES
        offset = block_entries - window_ids * SAMPLES
        following = jnp.minimum(window_ids + 1, windows - 1)
        paired = jnp.concatenate(
            [jnp.take(table, window_ids, axis=0), jnp.take(table, following, axis=0)], axis=1
        )
        for level in range(shift_bits):
            moved_by = (1 << level) * feat_count
            moved = jnp.concatenate(
                [paired[:, moved_by:], jnp.zeros((block, moved_by), paired.dtype)], axis=1
            )
            taken = (offset >> level & 1)[:, None] == 1
            paired = jnp.where(taken, moved, paired)
        probed_values = paired[:, :span].reshape(block, SAMPLES, feat_count)
        before_activation = jnp.einsum(
            "fh,isf->hsi", input_layer_weight, probed_values, preferred_element_type=jnp.float32
        )
        hidden = (
            jnp.maximum(before_activation, 0.0).astype(jnp.bfloat16).reshape(-1, SAMPLES * block)
        )
        field = jnp.einsum("ho,hn->on", second_weight, hidden, preferred_element_type=jnp.float32)
        return blend_sample_values(field.reshape(-1, SAMPLES, block), block_counts, bricks)

    colour_blocks, depth_blocks = lax.map(
        march_block, (entries.reshape(-1, block), counts.reshape(-1, block))
    )
    colour = jnp.transpose(colour_blocks, (1, 0, 2)).reshape(colour_blocks.shape[1], total_rays)
    depth_sum = depth_blocks.reshape(1, total_rays)
    all_depth = lax.all_gather(depth_sum, "depth", axis=0, tiled=True)
    my_rank = ranks[lax.axis_index("depth")]
    ahead = (ranks < my_rank).astype(jnp.float32)[None, :]
    front = jnp.dot(ahead, all_depth, precision=lax.Precision.HIGHEST)
    image = lax.psum_scatter(
        (colour * jnp.exp(-front)).astype(jnp.bfloat16), "depth", scatter_dimension=1, tiled=True
    ).astype(jnp.float32)
    image = image.reshape(-1, ROWS_OWN, COLS_DEV).transpose(1, 2, 0).astype(jnp.bfloat16)
    first = jnp.maximum(convolve_valid(border_padding(image), conv_in), 0.0).astype(jnp.bfloat16)
    second = jnp.maximum(convolve_valid(border_padding(first), conv_mid), 0.0).astype(jnp.bfloat16)
    frame = convolve_valid(border_padding(second), conv_out).astype(jnp.bfloat16)
    return frame


def solution(mesh):
    placed = (
        P(None, ("groups", "depth"), "rays", None),
        P(("groups", "depth"), "rays", None),
        P(("groups", "depth"), "rays", None),
        P(("groups", "rays"), None),
        P(),
        P(),
        P(),
        P(),
        P(),
    )
    return jax.shard_map(
        shards,
        mesh=mesh,
        in_specs=placed,
        out_specs=P(("groups", "depth"), "rays", None),
        check_vma=False,
    )
```

profile of v0, /device:TPU:1, one launch (start us, length us, event | category | flops | bytes accessed | tf_op | source)
XLA Modules:
  0.0 133.9 jit_solution(3947614905401499600)
XLA Ops:
  7.1 1.3 reduce.10
  8.3 1.3 reduce.11
  9.6 5.4 %reshape.274 = bf16[16,1024,16]{2,1,0:T(8,128)(2,1)} reshape(bf16[16,1,1,16384]{3,0,2,1:T(8,128)(2,1)} %param.13) | data formatting | bytes 1048576 | tf_op jit(solution)/shard_map/reshape | solution.py:72
  15.1 3.7 %copy.18 = bf16[1024,16,16]{0,2,1:T(8,128)(2,1)S(1)} copy(bf16[1024,16,16]{1,0,2:T(8,128)(2,1)} %bitcast.218) | data formatting | bytes 1048576 | tf_op jit(solution)/shard_map/transpose | solution.py:73
  19.0 19.6 %while.14 = (s32[]{:T(128)}, f32[2,32,512]{2,1,0:T(8,128)S(1)}, f32[2,512]{1,0:T(2,128)S(1)}, s32[2,512]{1,0:T(2,128)S(1)}, s32[2,512]{1,0:T(2,128)S(1)}, /*inde...) while((s32[]{:T(128)}, f32[2,32,512]{2,1,0:T(8,128)S(1)}, ...), condition=%wide.region_3.5_spmd, body=%wide.region_0.4_spmd.sunk | while | flops 110472448 | bytes 23171440 | solution.py:108
  19.1 2.0 %gather_fusion.1 = bf16[512,256]{1,0:T(8,128)(2,1)S(1)} fusion(bf16[1024,256]{1,0:T(8,128)(2,1)S(1)} %get-tuple-element.298, s32[1024]{0:T(1024)S(1)} %pad_clamp_fusion.5), kind=kCustom, calls=%fused_computation.clone.clone.1 | custom fusion | bytes 526336 | tf_op jit(solution)/shard_map/while/body/eval_jaxpr/jit(_take)/gather | solution.py:89
  21.2 2.0 %gather_fusion = bf16[512,256]{1,0:T(8,128)(2,1)S(1)} fusion(bf16[1024,256]{1,0:T(8,128)(2,1)S(1)} %get-tuple-element.298, s32[1024]{0:T(1024)S(1)} %pad_clamp_fusion.4), kind=kCustom, calls=%fused_computation.1.clone.clone.1 | custom fusion | bytes 526336 | tf_op jit(solution)/shard_map/while/body/eval_jaxpr/jit(_take)/gather | solution.py:89
  26.1 1.3 convolution_bitcast_fusion.2
  28.9 2.0 %gather_fusion.1 = bf16[512,256]{1,0:T(8,128)(2,1)S(1)} fusion(bf16[1024,256]{1,0:T(8,128)(2,1)S(1)} %get-tuple-element.298, s32[1024]{0:T(1024)S(1)} %pad_clamp_fusion.5), kind=kCustom, calls=%fused_computation.clone.clone.1 | custom fusion | bytes 526336 | tf_op jit(solution)/shard_map/while/body/eval_jaxpr/jit(_take)/gather | solution.py:89
  31.0 2.0 %gather_fusion = bf16[512,256]{1,0:T(8,128)(2,1)S(1)} fusion(bf16[1024,256]{1,0:T(8,128)(2,1)S(1)} %get-tuple-element.298, s32[1024]{0:T(1024)S(1)} %pad_clamp_fusion.4), kind=kCustom, calls=%fused_computation.1.clone.clone.1 | custom fusion | bytes 526336 | tf_op jit(solution)/shard_map/while/body/eval_jaxpr/jit(_take)/gather | solution.py:89
  35.9 1.3 convolution_bitcast_fusion.2
  38.6 11.3 %all-gather = f32[4,1,1024]{2,1,0:T(1,128)S(1)} all-gather(f32[1,1,1024]{2,1,0:T(1,128)S(1)} %reshape.322), channel_id=1, replica_groups=mesh['groups'=2,'depth'=4,'rays'=4] {'depth'}, dimensions={0}, use_global_device_ids=true | all-gather | bytes 20480 | tf_op jit(solution)/shard_map/all_gather | solution.py:113
  52.0 20.8 %reduce-scatter.2.cloned.1.call-done = bf16[32,256]{1,0:T(8,128)(2,1)} async-done(((bf16[32,1024]{1,0:T(8,128)(2,1)}), bf16[32,256]{1,0:T(8,128)(2,1)}) %reduce-scatter.2.cloned.1.call-update) | async-done | bytes 16400 | tf_op jit(solution)/shard_map/reduce_scatter | solution.py:117
  72.8 0.8 copy.21
  73.6 1.3 collective-permute-start
  74.9 1.3 collective-permute-start.1
  76.2 3.0 %collective-permute-done.1 = bf16[1,16,32]{2,1,0:T(8,128)(2,1)S(1)} collective-permute-done((bf16[1,16,32]{2,1,0:T(8,128)(2,1)S(1)}, bf16[1,16,32]{2,1,0:T(8,128)(2,1)S(1)}, u32[]{:S(2)}, u32[]{:S(2)}) %collective-permute-start.1) | collective-permute-done | bytes 1056 | tf_op jit(solution)/shard_map/ppermute | solution.py:21
  79.3 7.1 %collective-permute-start.2 = (bf16[18,1,32]{2,1,0:T(2,128)(2,1)S(1)}, bf16[18,1,32]{2,1,0:T(2,128)(2,1)S(1)}, u32[]{:S(2)}, u32[]{:S(2)}) collective-permute-start(bf16[18,1,32]{2,1,0:T(2,128)(2,1)S(1)} %get-tuple-element.183), channel_id=1, source_target_pairs={{0,1},{1,2},{2,3},{4,5},{5,6},{6,7},{8,9},{9,10},{10,11},{12,13},{... | collective-permute-start | bytes 3464 | tf_op jit(solution)/shard_map/ppermute | solution.py:20
  86.4 1.9 %collective-permute-start.3 = (bf16[18,1,32]{2,1,0:T(2,128)(2,1)S(1)}, bf16[18,1,32]{2,1,0:T(2,128)(2,1)S(1)}, u32[]{:S(2)}, u32[]{:S(2)}) collective-permute-start(bf16[18,1,32]{2,1,0:T(2,128)(2,1)S(1)} %get-tuple-element.184), channel_id=1, source_target_pairs={{1,0},{2,1},{3,2},{5,4},{6,5},{7,6},{9,8},{10,9},{11,10},{13,12},{... | collective-permute-start | bytes 3464 | tf_op jit(solution)/shard_map/ppermute | solution.py:21
  88.5 2.9 %collective-permute-done.3 = bf16[18,1,32]{2,1,0:T(2,128)(2,1)S(1)} collective-permute-done((bf16[18,1,32]{2,1,0:T(2,128)(2,1)S(1)}, bf16[18,1,32]{2,1,0:T(2,128)(2,1)S(1)}, u32[]{:S(2)}, u32[]{:S(2)}) %collective-permute-start.3) | collective-permute-done | bytes 1184 | tf_op jit(solution)/shard_map/ppermute | solution.py:21
  92.7 3.4 %collective-permute-start.4 = (bf16[1,16,128]{2,1,0:T(8,128)(2,1)S(1)}, bf16[1,16,128]{2,1,0:T(8,128)(2,1)S(1)}, u32[]{:S(2)}, u32[]{:S(2)}) collective-permute-start(bf16[1,16,128]{2,1,0:T(8,128)(2,1)S(1)} %get-tuple-element.191), channel_id=1, source_target_pairs={{0,4},{4,8},{8,12},{1,5},{5,9},{9,13},{2,6},{6,10},{10,14},{3,7},{... | collective-permute-start | bytes 12296 | tf_op jit(solution)/shard_map/ppermute | solution.py:20
  96.1 1.3 collective-permute-start.5
  97.4 3.0 %collective-permute-done.5 = bf16[1,16,128]{2,1,0:T(8,128)(2,1)S(1)} collective-permute-done((bf16[1,16,128]{2,1,0:T(8,128)(2,1)S(1)}, bf16[1,16,128]{2,1,0:T(8,128)(2,1)S(1)}, u32[]{:S(2)}, u32[]{:S(2)}) %collective-permute-start.5) | collective-permute-done | bytes 4128 | tf_op jit(solution)/shard_map/ppermute | solution.py:21
  100.4 3.4 %collective-permute-start.6 = (bf16[18,1,128]{2,1,0:T(2,128)(2,1)S(1)}, bf16[18,1,128]{2,1,0:T(2,128)(2,1)S(1)}, u32[]{:S(2)}, u32[]{:S(2)}) collective-permute-start(bf16[18,1,128]{2,1,0:T(2,128)(2,1)S(1)} %get-tuple-element.179), channel_id=1, source_target_pairs={{0,1},{1,2},{2,3},{4,5},{5,6},{6,7},{8,9},{9,10},{10,11},{12,13},{... | collective-permute-start | bytes 13832 | tf_op jit(solution)/shard_map/ppermute | solution.py:20
  103.8 1.9 %collective-permute-start.7 = (bf16[18,1,128]{2,1,0:T(2,128)(2,1)S(1)}, bf16[18,1,128]{2,1,0:T(2,128)(2,1)S(1)}, u32[]{:S(2)}, u32[]{:S(2)}) collective-permute-start(bf16[18,1,128]{2,1,0:T(2,128)(2,1)S(1)} %get-tuple-element.180), channel_id=1, source_target_pairs={{1,0},{2,1},{3,2},{5,4},{6,5},{7,6},{9,8},{10,9},{11,10},{13,12},{... | collective-permute-start | bytes 13832 | tf_op jit(solution)/shard_map/ppermute | solution.py:21
  106.0 2.9 %collective-permute-done.7 = bf16[18,1,128]{2,1,0:T(2,128)(2,1)S(1)} collective-permute-done((bf16[18,1,128]{2,1,0:T(2,128)(2,1)S(1)}, bf16[18,1,128]{2,1,0:T(2,128)(2,1)S(1)}, u32[]{:S(2)}, u32[]{:S(2)}) %collective-permute-start.7) | collective-permute-done | bytes 4640 | tf_op jit(solution)/shard_map/ppermute | solution.py:21
  110.2 2.1 %collective-permute-start.8 = (bf16[1,16,128]{2,1,0:T(8,128)(2,1)S(1)}, bf16[1,16,128]{2,1,0:T(8,128)(2,1)S(1)}, u32[]{:S(2)}, u32[]{:S(2)}) collective-permute-start(bf16[1,16,128]{2,1,0:T(8,128)(2,1)S(1)} %get-tuple-element.187), channel_id=1, source_target_pairs={{0,4},{4,8},{8,12},{1,5},{5,9},{9,13},{2,6},{6,10},{10,14},{3,7},{... | collective-permute-start | bytes 12296 | tf_op jit(solution)/shard_map/ppermute | solution.py:20
  112.3 1.3 collective-permute-start.9
  113.6 3.0 %collective-permute-done.9 = bf16[1,16,128]{2,1,0:T(8,128)(2,1)S(1)} collective-permute-done((bf16[1,16,128]{2,1,0:T(8,128)(2,1)S(1)}, bf16[1,16,128]{2,1,0:T(8,128)(2,1)S(1)}, u32[]{:S(2)}, u32[]{:S(2)}) %collective-permute-start.9) | collective-permute-done | bytes 4128 | tf_op jit(solution)/shard_map/ppermute | solution.py:21
  116.7 3.4 %collective-permute-start.10 = (bf16[18,1,128]{2,1,0:T(2,128)(2,1)S(1)}, bf16[18,1,128]{2,1,0:T(2,128)(2,1)S(1)}, u32[]{:S(2)}, u32[]{:S(2)}) collective-permute-start(bf16[18,1,128]{2,1,0:T(2,128)(2,1)S(1)} %get-tuple-element.175), channel_id=1, source_target_pairs={{0,1},{1,2},{2,3},{4,5},{5,6},{6,7},{8,9},{9,10},{10,11},{12,13},{... | collective-permute-start | bytes 13832 | tf_op jit(solution)/shard_map/ppermute | solution.py:20
  120.1 1.9 %collective-permute-start.11 = (bf16[18,1,128]{2,1,0:T(2,128)(2,1)S(1)}, bf16[18,1,128]{2,1,0:T(2,128)(2,1)S(1)}, u32[]{:S(2)}, u32[]{:S(2)}) collective-permute-start(bf16[18,1,128]{2,1,0:T(2,128)(2,1)S(1)} %get-tuple-element.176), channel_id=1, source_target_pairs={{1,0},{2,1},{3,2},{5,4},{6,5},{7,6},{9,8},{10,9},{11,10},{13,12},{... | collective-permute-start | bytes 13832 | tf_op jit(solution)/shard_map/ppermute | solution.py:21
  122.2 2.9 %collective-permute-done.11 = bf16[18,1,128]{2,1,0:T(2,128)(2,1)S(1)} collective-permute-done((bf16[18,1,128]{2,1,0:T(2,128)(2,1)S(1)}, bf16[18,1,128]{2,1,0:T(2,128)(2,1)S(1)}, u32[]{:S(2)}, u32[]{:S(2)}) %collective-permute-start.11) | collective-permute-done | bytes 4640 | tf_op jit(solution)/shard_map/ppermute | solution.py:21
  (132 shorter events, 16.5 us)
Async XLA Ops:
  6.5 66.3 %reduce-scatter.2.cloned.1.call-start = ((), (), s32[]{:S(2)}) async-start(), calls=%async_computation.1 | async-start | bytes 81920 | tf_op jit(solution)/shard_map/reduce_scatter | solution.py:117
  15.1 3.9 %copy-start.2 = (bf16[128,33]{0,1:T(8,128)(2,1)S(1)}, bf16[128,33]{0,1:T(8,128)(2,1)}, u32[]{:S(2)}) copy-start(bf16[128,33]{0,1:T(8,128)(2,1)} %param.18) | copy-start | bytes 25348
  15.1 3.9 %copy-start.3 = (bf16[16,128]{1,0:T(8,128)(2,1)S(1)}, bf16[16,128]{1,0:T(8,128)(2,1)}, u32[]{:S(2)}) copy-start(bf16[16,128]{1,0:T(8,128)(2,1)} %param.17) | copy-start | bytes 12292
  19.0 30.9 %copy-start.5 = (s32[1,4]{1,0:T(1,128)S(1)}, s32[1,4]{1,0:T(1,128)}, u32[]{:S(2)}) copy-start(s32[1,4]{1,0:T(1,128)} %param.16) | copy-start | bytes 52
  19.0 69.4 %copy-start.4 = (bf16[9,32,128]{2,1,0:T(8,128)(2,1)S(1)}, bf16[9,32,128]{2,1,0:T(8,128)(2,1)}, u32[]{:S(2)}) copy-start(bf16[9,32,128]{2,1,0:T(8,128)(2,1)} %param.19) | copy-start | bytes 221188
  73.6 2.6 %collective-permute-start = (bf16[1,16,32]{2,1,0:T(8,128)(2,1)S(1)}, bf16[1,16,32]{2,1,0:T(8,128)(2,1)S(1)}, u32[]{:S(2)}, u32[]{:S(2)}) collective-permute-start(bf16[1,16,32]{2,1,0:T(8,128)(2,1)S(1)} %get-tuple-element.195), channel_id=1, source_target_pairs={{0,4},{4,8},{8,12},{1,5},{5,9},{9,13},{2,6},{6,10},{10,14},{3,7},{... | collective-permute-start | bytes 3080 | tf_op jit(solution)/shard_map/ppermute | solution.py:20
  74.9 4.4 %collective-permute-start.1 = (bf16[1,16,32]{2,1,0:T(8,128)(2,1)S(1)}, bf16[1,16,32]{2,1,0:T(8,128)(2,1)S(1)}, u32[]{:S(2)}, u32[]{:S(2)}) collective-permute-start(bf16[1,16,32]{2,1,0:T(8,128)(2,1)S(1)} %get-tuple-element.196), channel_id=1, source_target_pairs={{4,0},{8,4},{12,8},{5,1},{9,5},{13,9},{6,2},{10,6},{14,10},{7,3},{... | collective-permute-start | bytes 3080 | tf_op jit(solution)/shard_map/ppermute | solution.py:21
  79.3 9.2 %collective-permute-start.2 = (bf16[18,1,32]{2,1,0:T(2,128)(2,1)S(1)}, bf16[18,1,32]{2,1,0:T(2,128)(2,1)S(1)}, u32[]{:S(2)}, u32[]{:S(2)}) collective-permute-start(bf16[18,1,32]{2,1,0:T(2,128)(2,1)S(1)} %get-tuple-element.183), channel_id=1, source_target_pairs={{0,1},{1,2},{2,3},{4,5},{5,6},{6,7},{8,9},{9,10},{10,11},{12,13},{... | collective-permute-start | bytes 3464 | tf_op jit(solution)/shard_map/ppermute | solution.py:20
  86.4 5.0 %collective-permute-start.3 = (bf16[18,1,32]{2,1,0:T(2,128)(2,1)S(1)}, bf16[18,1,32]{2,1,0:T(2,128)(2,1)S(1)}, u32[]{:S(2)}, u32[]{:S(2)}) collective-permute-start(bf16[18,1,32]{2,1,0:T(2,128)(2,1)S(1)} %get-tuple-element.184), channel_id=1, source_target_pairs={{1,0},{2,1},{3,2},{5,4},{6,5},{7,6},{9,8},{10,9},{11,10},{13,12},{... | collective-permute-start | bytes 3464 | tf_op jit(solution)/shard_map/ppermute | solution.py:21
  88.4 17.4 %copy-start = (bf16[9,128,128]{2,1,0:T(8,128)(2,1)S(1)}, bf16[9,128,128]{2,1,0:T(8,128)(2,1)}, u32[]{:S(2)}) copy-start(bf16[9,128,128]{2,1,0:T(8,128)(2,1)} %param.20) | copy-start | bytes 884740
  92.7 4.7 %collective-permute-start.4 = (bf16[1,16,128]{2,1,0:T(8,128)(2,1)S(1)}, bf16[1,16,128]{2,1,0:T(8,128)(2,1)S(1)}, u32[]{:S(2)}, u32[]{:S(2)}) collective-permute-start(bf16[1,16,128]{2,1,0:T(8,128)(2,1)S(1)} %get-tuple-element.191), channel_id=1, source_target_pairs={{0,4},{4,8},{8,12},{1,5},{5,9},{9,13},{2,6},{6,10},{10,14},{3,7},{... | collective-permute-start | bytes 12296 | tf_op jit(solution)/shard_map/ppermute | solution.py:20
  96.1 4.4 %collective-permute-start.5 = (bf16[1,16,128]{2,1,0:T(8,128)(2,1)S(1)}, bf16[1,16,128]{2,1,0:T(8,128)(2,1)S(1)}, u32[]{:S(2)}, u32[]{:S(2)}) collective-permute-start(bf16[1,16,128]{2,1,0:T(8,128)(2,1)S(1)} %get-tuple-element.192), channel_id=1, source_target_pairs={{4,0},{8,4},{12,8},{5,1},{9,5},{13,9},{6,2},{10,6},{14,10},{7,3},{... | collective-permute-start | bytes 12296 | tf_op jit(solution)/shard_map/ppermute | solution.py:21
  100.4 5.5 %collective-permute-start.6 = (bf16[18,1,128]{2,1,0:T(2,128)(2,1)S(1)}, bf16[18,1,128]{2,1,0:T(2,128)(2,1)S(1)}, u32[]{:S(2)}, u32[]{:S(2)}) collective-permute-start(bf16[18,1,128]{2,1,0:T(2,128)(2,1)S(1)} %get-tuple-element.179), channel_id=1, source_target_pairs={{0,1},{1,2},{2,3},{4,5},{5,6},{6,7},{8,9},{9,10},{10,11},{12,13},{... | collective-permute-start | bytes 13832 | tf_op jit(solution)/shard_map/ppermute | solution.py:20
  103.8 5.0 %collective-permute-start.7 = (bf16[18,1,128]{2,1,0:T(2,128)(2,1)S(1)}, bf16[18,1,128]{2,1,0:T(2,128)(2,1)S(1)}, u32[]{:S(2)}, u32[]{:S(2)}) collective-permute-start(bf16[18,1,128]{2,1,0:T(2,128)(2,1)S(1)} %get-tuple-element.180), channel_id=1, source_target_pairs={{1,0},{2,1},{3,2},{5,4},{6,5},{7,6},{9,8},{10,9},{11,10},{13,12},{... | collective-permute-start | bytes 13832 | tf_op jit(solution)/shard_map/ppermute | solution.py:21
  105.9 16.1 %copy-start.1 = (bf16[9,128,128]{2,1,0:T(8,128)(2,1)S(1)}, bf16[9,128,128]{2,1,0:T(8,128)(2,1)}, u32[]{:S(2)}) copy-start(bf16[9,128,128]{2,1,0:T(8,128)(2,1)} %param.21) | copy-start | bytes 884740
  110.2 3.5 %collective-permute-start.8 = (bf16[1,16,128]{2,1,0:T(8,128)(2,1)S(1)}, bf16[1,16,128]{2,1,0:T(8,128)(2,1)S(1)}, u32[]{:S(2)}, u32[]{:S(2)}) collective-permute-start(bf16[1,16,128]{2,1,0:T(8,128)(2,1)S(1)} %get-tuple-element.187), channel_id=1, source_target_pairs={{0,4},{4,8},{8,12},{1,5},{5,9},{9,13},{2,6},{6,10},{10,14},{3,7},{... | collective-permute-start | bytes 12296 | tf_op jit(solution)/shard_map/ppermute | solution.py:20
  112.3 4.4 %collective-permute-start.9 = (bf16[1,16,128]{2,1,0:T(8,128)(2,1)S(1)}, bf16[1,16,128]{2,1,0:T(8,128)(2,1)S(1)}, u32[]{:S(2)}, u32[]{:S(2)}) collective-permute-start(bf16[1,16,128]{2,1,0:T(8,128)(2,1)S(1)} %get-tuple-element.188), channel_id=1, source_target_pairs={{4,0},{8,4},{12,8},{5,1},{9,5},{13,9},{6,2},{10,6},{14,10},{7,3},{... | collective-permute-start | bytes 12296 | tf_op jit(solution)/shard_map/ppermute | solution.py:21
  116.7 5.5 %collective-permute-start.10 = (bf16[18,1,128]{2,1,0:T(2,128)(2,1)S(1)}, bf16[18,1,128]{2,1,0:T(2,128)(2,1)S(1)}, u32[]{:S(2)}, u32[]{:S(2)}) collective-permute-start(bf16[18,1,128]{2,1,0:T(2,128)(2,1)S(1)} %get-tuple-element.175), channel_id=1, source_target_pairs={{0,1},{1,2},{2,3},{4,5},{5,6},{6,7},{8,9},{9,10},{10,11},{12,13},{... | collective-permute-start | bytes 13832 | tf_op jit(solution)/shard_map/ppermute | solution.py:20
  120.1 5.0 %collective-permute-start.11 = (bf16[18,1,128]{2,1,0:T(2,128)(2,1)S(1)}, bf16[18,1,128]{2,1,0:T(2,128)(2,1)S(1)}, u32[]{:S(2)}, u32[]{:S(2)}) collective-permute-start(bf16[18,1,128]{2,1,0:T(2,128)(2,1)S(1)} %get-tuple-element.176), channel_id=1, source_target_pairs={{1,0},{2,1},{3,2},{5,4},{6,5},{7,6},{9,8},{10,9},{11,10},{13,12},{... | collective-permute-start | bytes 13832 | tf_op jit(solution)/shard_map/ppermute | solution.py:21
Sparse Core Ops, SparseCore 0:
  52.1 20.6 reduce-scatter.1
where the time goes:
time: 135 us; the launch traced here: 134 us
  waiting for transfers between devices  38.6 us (29%)
  starting transfers between devices  30.3 us (22%)
  local copies, waits for them, and re-layouts  22.4 us (17%)
  between operations  13.9 us (10%)
  blocking collectives  11.3 us (8%)
  matrix products  9.79 us (7%)
  other arithmetic  7.22 us (5%)
    reduce_scatter x1, waiting for transfers between devices, shards(): lax.psum_scatter((colour * jnp.exp(-front)).astype(jnp.bfloat16), 'depth'...  20.8 us
    ppermute x6, starting transfers between devices, padded_2(): before = lax.ppermute(last, axis, up)  20.7 us
    ppermute x6, waiting for transfers between devices, padded_2(): after = lax.ppermute(first, axis, down)  17.7 us
    all_gather x1, blocking collectives, shards(): all_depth = lax.all_gather(depth_sum, 'depth', axis=0, tiled=True)  11.3 us
    ppermute x6, starting transfers between devices, padded_2(): after = lax.ppermute(first, axis, down)  9.64 us
    reshape x1, local copies, waits for them, and re-layouts, shards(): brick_features.reshape(feat_count, windows, SAMPLES).transpose(1, 2, 0)  5.43 us
    dot_general x27, matrix products, convolve_valid(): jnp.dot(window, weights[tap], preferred_element_type=jnp.float32)  4.52 us
    gather x2, local copies, waits for them, and re-layouts, march_block(): jnp.take(table, window_ids, axis=0)  3.91 us
  transfers between devices with their start and end apart: 13, of which 7 were waited for; matrix products, arithmetic and copies ran while one was open for 0% of the time, Pallas kernels for 0%

commit v1 on v0

--- a/solution.py
+++ b/solution.py
@@ -1,26 +1,20 @@
+import functools
 import math
 
 import jax
 import jax.numpy as jnp
 from jax import lax
+from jax.experimental import pallas as pl
+from jax.experimental.pallas import tpu as pltpu
 from jax.sharding import PartitionSpec as P
 
 SAMPLES = 16
 ROWS_OWN = 16
 COLS_DEV = 16
-
-
-def padded_2(x, sides, width):
-    for axis, dim in sides:
-        size, length = (lax.axis_size(axis), x.shape[dim])
-        up = [(i, (i + 1) % size) for i in range(size - 1)]
-        down = [(j, i) for i, j in up]
-        last = lax.slice_in_dim(x, length - width, length, axis=dim)
-        first = lax.slice_in_dim(x, 0, width, axis=dim)
-        before = lax.ppermute(last, axis, up)
-        after = lax.ppermute(first, axis, down)
-        x = jnp.concatenate([before, x, after], axis=dim)
-    return x
+HALO = 4
+MESSAGE = (ROWS_OWN + 2 * HALO) * COLS_DEV
+WIDE = 2 * COLS_DEV
+MESH = pl.DeviceIdType.MESH
 
 
 def blend_sample_values(field, counts, bricks):
@@ -35,21 +29,234 @@
     return (colour, jnp.sum(optical, axis=0))
 
 
-def convolve_valid(padded, weights):
-    height = padded.shape[0] - 2
-    width = padded.shape[1] - 2
-    total = jnp.zeros((height * width, weights.shape[2]), jnp.float32)
+def composite_head(
+    bricks,
+    tiles,
+    ahead_ref,
+    colour_ref,
+    depth_ref,
+    conv_in_ref,
+    conv_mid_ref,
+    conv_out_ref,
+    frame_ref,
+    depths,
+    outbox,
+    inbox,
+    strip,
+    beside,
+    depth_send,
+    depth_recv,
+    part_send,
+    part_recv,
+    side_send,
+    side_recv,
+):
+    me = lax.axis_index("depth")
+    tile = lax.axis_index("rays")
+    channels = colour_ref.shape[0]
+    rays = colour_ref.shape[1]
+    height = rays // COLS_DEV
+    width = tiles * COLS_DEV
+    peers = [lax.rem(me + step, bricks) for step in range(1, bricks)]
+
+    beside[...] = jnp.zeros_like(beside)
+    depths[me] = depth_ref[...]
+    barrier = pltpu.get_barrier_semaphore()
+    for peer in peers:
+        pl.semaphore_signal(barrier, inc=1, device_id={"depth": peer}, device_id_type=MESH)
+
+    @pl.when(tile > 0)
+    def _():
+        pl.semaphore_signal(barrier, inc=1, device_id={"rays": tile - 1}, device_id_type=MESH)
+
+    @pl.when(tile < tiles - 1)
+    def _():
+        pl.semaphore_signal(barrier, inc=1, device_id={"rays": tile + 1}, device_id_type=MESH)
+
+    lefts = lax.div(tile + tiles - 1, tiles)
+    rights = lax.div(2 * tiles - 2 - tile, tiles)
+    pl.semaphore_wait(barrier, bricks - 1 + lefts + rights)
+
+    def depth_copy(peer, slot):
+        return pltpu.make_async_remote_copy(
+            src_ref=depth_ref,
+            dst_ref=depths.at[slot],
+            send_sem=depth_send.at[peer],
+            recv_sem=depth_recv.at[slot],
+            device_id={"depth": peer},
+            device_id_type=MESH,
+        )
+
+    for peer in peers:
+        depth_copy(peer, me).start()
+    for peer in peers:
+        depth_copy(peer, peer).wait_recv()
+    front = jnp.zeros_like(depth_ref)
+    for brick in range(bricks):
+        front = front + ahead_ref[brick] * depths[brick]
+    dimmed = (colour_ref[...] * jnp.exp(-front)).astype(jnp.bfloat16).astype(jnp.float32)
+    margin = jnp.zeros((channels, HALO * COLS_DEV), jnp.float32)
+    outbox[...] = jnp.concatenate([margin, dimmed, margin], axis=1).astype(jnp.bfloat16)
+
+    def rows_of(owner):
+        start = pl.multiple_of(owner * (ROWS_OWN * COLS_DEV), ROWS_OWN * COLS_DEV)
+        return pl.ds(start, MESSAGE)
+
+    def part_copy(peer, slot):
+        return pltpu.make_async_remote_copy(
+            src_ref=outbox.at[:, rows_of(peer)],
+            dst_ref=inbox.at[slot],
+            send_sem=part_send.at[peer],
+            recv_sem=part_recv.at[slot],
+            device_id={"depth": peer},
+            device_id_type=MESH,
+        )
+
+    for peer in peers:
+        part_copy(peer, me).start()
+    inbox[me] = outbox[:, rows_of(me)]
+    for peer in peers:
+        part_copy(peer, peer).wait_recv()
+    total = jnp.zeros((channels, MESSAGE), jnp.float32)
+    for brick in range(bricks):
+        total = total + inbox[brick].astype(jnp.float32)
+    strip[...] = total.astype(jnp.bfloat16)
+
+    def side_copy(side):
+        return pltpu.make_async_remote_copy(
+            src_ref=strip,
+            dst_ref=beside.at[side],
+            send_sem=side_send.at[side],
+            recv_sem=side_recv.at[side],
+            device_id={"rays": tile + 1 - 2 * side},
+            device_id_type=MESH,
+        )
+
+    @pl.when(tile < tiles - 1)
+    def _():
+        side_copy(0).start()
+
+    @pl.when(tile > 0)
+    def _():
+        side_copy(1).start()
+
+    @pl.when(tile > 0)
+    def _():
+        side_copy(0).wait_recv()
+
+    @pl.when(tile < tiles - 1)
+    def _():
+        side_copy(1).wait_recv()
+
+    rows_in = ROWS_OWN + 2 * HALO
+    half = COLS_DEV // 2
+
+    def pixels(values):
+        return jnp.transpose(values.astype(jnp.float32)).reshape(rows_in, COLS_DEV, channels)
+
+    own = pixels(strip[...])
+    left = pixels(beside[0])
+    right = pixels(beside[1])
+    image = jnp.concatenate([left[:, half:], own, right[:, :half]], axis=1)
+    image = image.reshape(rows_in * WIDE, channels)
+
+    def shifted(flat):
+        count = flat.shape[0]
+        return [
+            pltpu.roll(flat, 1, 0).astype(jnp.bfloat16),
+            flat.astype(jnp.bfloat16),
+            pltpu.roll(flat, count - 1, 0).astype(jnp.bfloat16),
+        ]
+
+    def inside(first_row, count):
+        index = lax.broadcasted_iota(jnp.int32, (count * WIDE, 1), 0)
+        row = index // WIDE + (me * ROWS_OWN + first_row)
+        column = index % WIDE + (tile * COLS_DEV - half)
+        return (row >= 0) & (row < height) & (column >= 0) & (column < width)
+
+    moved = shifted(image)
+    count = ROWS_OWN + 4
+    first = jnp.zeros((count * WIDE, conv_in_ref.shape[2]), jnp.float32)
     for tap in range(9):
-        row_offset_shift, shift_col = divmod(tap, 3)
-        window = padded[
-            row_offset_shift : row_offset_shift + height, shift_col : shift_col + width
-        ].reshape(height * width, -1)
-        total = total + jnp.dot(window, weights[tap], preferred_element_type=jnp.float32)
-    return total.reshape(height, width, weights.shape[2])
-
-
-def border_padding(source):
-    return padded_2(source, (("depth", 0), ("rays", 1)), 1)
+        row, column = divmod(tap, 3)
+        begin = (HALO - 3 + row) * WIDE
+        first = first + jnp.dot(
+            moved[column][begin : begin + count * WIDE],
+            conv_in_ref[tap],
+            preferred_element_type=jnp.float32,
+        )
+    first = jnp.where(inside(-2, count), jnp.maximum(first, 0.0), 0.0)
+
+    def convolve(flat, weights, count):
+        joined = jnp.concatenate(shifted(flat), axis=1)
+        total = None
+        for row in range(3):
+            part = jnp.dot(
+                joined[row * WIDE : (row + count) * WIDE],
+                weights[row],
+                preferred_element_type=jnp.float32,
+            )
+            total = part if total is None else total + part
+        return total
+
+    count = ROWS_OWN + 2
+    second = convolve(first, conv_mid_ref, count)
+    second = jnp.where(inside(-1, count), jnp.maximum(second, 0.0), 0.0)
+    frame = convolve(second, conv_out_ref, ROWS_OWN)
+    frame = frame.reshape(ROWS_OWN, WIDE, frame.shape[1])[:, half : half + COLS_DEV]
+    frame_ref[...] = frame.astype(jnp.bfloat16)
+
+    for peer in peers:
+        depth_copy(peer, me).wait_send()
+    for peer in peers:
+        part_copy(peer, me).wait_send()
+
+    @pl.when(tile < tiles - 1)
+    def _():
+        side_copy(0).wait_send()
+
+    @pl.when(tile > 0)
+    def _():
+        side_copy(1).wait_send()
+
+
+def composite(ahead, colour, depth_sum, conv_in, conv_mid, conv_out):
+    bricks = lax.axis_size("depth")
+    tiles = lax.axis_size("rays")
+    channels, rays = colour.shape
+    outs = conv_in.shape[2]
+    vmem = pl.BlockSpec(memory_space=pltpu.VMEM)
+    dma = pltpu.SemaphoreType.DMA
+    return pl.pallas_call(
+        functools.partial(composite_head, bricks, tiles),
+        out_shape=jax.ShapeDtypeStruct((ROWS_OWN, COLS_DEV, outs), jnp.bfloat16),
+        in_specs=[pl.BlockSpec(memory_space=pltpu.SMEM)] + [vmem] * 5,
+        out_specs=vmem,
+        scratch_shapes=[
+            pltpu.VMEM((bricks, 1, rays), jnp.float32),
+            pltpu.VMEM((channels, rays + 2 * HALO * COLS_DEV), jnp.bfloat16),
+            pltpu.VMEM((bricks, channels, MESSAGE), jnp.bfloat16),
+            pltpu.VMEM((channels, MESSAGE), jnp.bfloat16),
+            pltpu.VMEM((2, channels, MESSAGE), jnp.bfloat16),
+            dma((bricks,)),
+            dma((bricks,)),
+            dma((bricks,)),
+            dma((bricks,)),
+            dma((2,)),
+            dma((2,)),
+        ],
+        compiler_params=pltpu.CompilerParams(
+            collective_id=0, has_side_effects=True, vmem_limit_bytes=48 * 1024 * 1024
+        ),
+        name="composite_head",
+    )(
+        ahead,
+        colour,
+        depth_sum,
+        conv_in,
+        conv_mid.reshape(3, -1, conv_mid.shape[2]),
+        conv_out.reshape(3, -1, conv_out.shape[2]),
+    )
 
 
 def shards(
@@ -110,18 +317,9 @@
     )
     colour = jnp.transpose(colour_blocks, (1, 0, 2)).reshape(colour_blocks.shape[1], total_rays)
     depth_sum = depth_blocks.reshape(1, total_rays)
-    all_depth = lax.all_gather(depth_sum, "depth", axis=0, tiled=True)
     my_rank = ranks[lax.axis_index("depth")]
-    ahead = (ranks < my_rank).astype(jnp.float32)[None, :]
-    front = jnp.dot(ahead, all_depth, precision=lax.Precision.HIGHEST)
-    image = lax.psum_scatter(
-        (colour * jnp.exp(-front)).astype(jnp.bfloat16), "depth", scatter_dimension=1, tiled=True
-    ).astype(jnp.float32)
-    image = image.reshape(-1, ROWS_OWN, COLS_DEV).transpose(1, 2, 0).astype(jnp.bfloat16)
-    first = jnp.maximum(convolve_valid(border_padding(image), conv_in), 0.0).astype(jnp.bfloat16)
-    second = jnp.maximum(convolve_valid(border_padding(first), conv_mid), 0.0).astype(jnp.bfloat16)
-    frame = convolve_valid(border_padding(second), conv_out).astype(jnp.bfloat16)
-    return frame
+    ahead = (ranks < my_rank).astype(jnp.float32)
+    return composite(ahead, colour, depth_sum, conv_in, conv_mid, conv_out)
 
 
 def solution(mesh):

time: 135 us -> 53.9 us (0.40)
  waiting for transfers between devices: 38.6 us -> 0 us
  starting transfers between devices: 30.3 us -> 0 us
  Pallas kernels: 0 us -> 18.1 us
  between operations: 13.9 us -> 0.14 us
  blocking collectives: 11.3 us -> 0 us
  matrix products: 9.79 us -> 4.49 us
    ppermute x12 -> x0, starting transfers between devices: 30.3 us -> none  [the longest x6 20.7 us: padded_2(): before = lax.ppermute(last, axis, up)]
    reduce_scatter x1 -> x0, waiting for transfers between devices: 20.8 us -> none  [shards(): lax.psum_scatter((colour * jnp.exp(-front)).astype(jnp.bfloat16), 'depth'...]
    pallas_call x0 -> x1, Pallas kernels: none -> 18.1 us  [composite(): pl.pallas_call(functools.partial(composite_head, bricks, tiles), out_shap...]
    ppermute x12 -> x0, waiting for transfers between devices: 17.7 us -> none  [the longest x6 17.7 us: padded_2(): after = lax.ppermute(first, axis, down)]
    all_gather x1 -> x0, blocking collectives: 11.3 us -> none  [shards(): all_depth = lax.all_gather(depth_sum, 'depth', axis=0, tiled=True)]
    dot_general x28 -> x0, matrix products: 5.3 us -> none  [the longest x27 4.52 us: convolve_valid(): jnp.dot(window, weights[tap], preferred_element_type=jnp.float32)]
  transfers between devices with their start and end apart: 13 -> 0, of which waited for: 7 -> 0; matrix products, arithmetic and copies ran while one was open for 0% -> 0% of each run, Pallas kernels for 0% -> 0%
where the time goes in v1:
time: 53.9 us; the launch traced here: 53.6 us
  local copies, waits for them, and re-layouts  22.7 us (42%)
  Pallas kernels  18.1 us (34%)
  other arithmetic  7.7 us (14%)
  matrix products  4.49 us (8%)
    pallas_call x1, Pallas kernels, composite(): pl.pallas_call(functools.partial(composite_head, bricks, tiles), out_shap...  18.1 us
    reshape x1, local copies, waits for them, and re-layouts, shards(): brick_features.reshape(feat_count, windows, SAMPLES).transpose(1, 2, 0)  5.42 us
    gather x2, local copies, waits for them, and re-layouts, march_block(): jnp.take(table, window_ids, axis=0)  3.91 us
    gather x2, local copies, waits for them, and re-layouts, march_block(): jnp.take(table, following, axis=0)  3.91 us
    transpose x1, local copies, waits for them, and re-layouts, shards(): table = brick_features.reshape(feat_count, windows, SAMPLES).transpose(1,...  3.68 us
    unnamed x2, other arithmetic  2.69 us
    dot_general x2, matrix products, march_block(): jnp.einsum('ho,hn->on', second_weight, hidden, preferred_element_type=jnp...  2.63 us
    select_n x8, other arithmetic, march_block(): paired = jnp.where(taken, moved, paired)  1.87 us

profile of v1, /device:TPU:1, one launch (start us, length us, event | category | flops | bytes accessed | tf_op | source)
XLA Modules:
  0.0 53.6 jit_solution(376074722153568449)
XLA Ops:
  0.0 1.2 %constant_dynamic-slice_fusion.2 = s32[1,1]{1,0:T(1,128)} fusion(s32[1,4]{1,0:T(1,128)} %param.16, s32[]{:T(128)S(6)} %select_n.78), kind=kLoop, calls=%fused_computation.52 | loop fusion | bytes 12 | tf_op jit(solution)/shard_map/dynamic_slice | solution.py:320
  1.2 1.3 %fusion.14.ahead_ref = f32[4]{0:T(128)S(1)} fusion(s32[1,4]{1,0:T(1,128)} %param.16, s32[]{:T(128)} %bitcast.9), kind=kLoop, calls=%fused_computation.51 | loop fusion | flops 8 | bytes 36 | tf_op jit(solution)/shard_map/convert_element_type | solution.py:321
  2.5 0.5 broadcast.419
  3.1 1.3 %reduce.10 = s32[1024]{0:T(1024)S(1)} reduce(s32[1,1,1024]{2,1,0:T(1,128)} %param.15, s32[]{:T(128)} %broadcast.419), dimensions={0,1}, to_apply=%param.15.reduce_sub_computation.3 | reduce | bytes 8196 | tf_op args[2]
  4.4 1.3 %reduce.11 = s32[1024]{0:T(1024)S(1)} reduce(s32[1,1,1024]{2,1,0:T(1,128)} %param.14, s32[]{:T(128)} %broadcast.419), dimensions={0,1}, to_apply=%param.14.reduce_sub_computation.3 | reduce | bytes 8196 | tf_op args[1]
  5.8 5.4 %reshape.184 = bf16[16,1024,16]{2,1,0:T(8,128)(2,1)} reshape(bf16[16,1,1,16384]{3,0,2,1:T(8,128)(2,1)} %param.13) | data formatting | bytes 1048576 | tf_op jit(solution)/shard_map/reshape | solution.py:279
  11.2 3.7 %copy.14 = bf16[1024,16,16]{0,2,1:T(8,128)(2,1)S(1)} copy(bf16[1024,16,16]{1,0,2:T(8,128)(2,1)} %bitcast.72) | data formatting | bytes 1048576 | tf_op jit(solution)/shard_map/transpose | solution.py:280
  15.2 19.5 %while.14 = (s32[]{:T(128)}, f32[2,32,512]{2,1,0:T(8,128)S(1)}, f32[2,512]{1,0:T(2,128)S(1)}, s32[2,512]{1,0:T(2,128)S(1)}, s32[2,512]{1,0:T(2,128)S(1)}, /*inde...) while((s32[]{:T(128)}, f32[2,32,512]{2,1,0:T(8,128)S(1)}, ...), condition=%wide.region_3.5_spmd, body=%wide.region_0.4_spmd.sunk | while | flops 110472448 | bytes 23171440 | solution.py:315
  15.2 2.0 %gather_fusion.1 = bf16[512,256]{1,0:T(8,128)(2,1)S(1)} fusion(bf16[1024,256]{1,0:T(8,128)(2,1)S(1)} %get-tuple-element.245, s32[1024]{0:T(1024)S(1)} %pad_clamp_fusion.5), kind=kCustom, calls=%fused_computation.clone.clone.1 | custom fusion | bytes 526336 | tf_op jit(solution)/shard_map/while/body/eval_jaxpr/jit(_take)/gather | solution.py:296
  17.4 2.0 %gather_fusion = bf16[512,256]{1,0:T(8,128)(2,1)S(1)} fusion(bf16[1024,256]{1,0:T(8,128)(2,1)S(1)} %get-tuple-element.245, s32[1024]{0:T(1024)S(1)} %pad_clamp_fusion.4), kind=kCustom, calls=%fused_computation.1.clone.clone.1 | custom fusion | bytes 526336 | tf_op jit(solution)/shard_map/while/body/eval_jaxpr/jit(_take)/gather | solution.py:296
  19.5 0.3 fusion.33
  19.8 0.3 fusion.34
  20.1 0.3 slice.82
  20.4 0.3 pad_select_fusion.4
  20.6 0.3 slice.83
  20.9 0.3 pad_select_fusion.5
  21.5 0.8 %maximum_convert_fusion.2 = bf16[512,16,128]{2,0,1:T(8,128)(2,1)S(1)} fusion(bf16[512,16,16]{0,2,1:T(8,128)(2,1)S(1)} %bitcast.71, bf16[16,128]{1,0:T(8,128)(2,1)S(1)} %get-tuple-element.246), kind=kOutput, calls=%fused_computation.3.clone.1 | convolution fusion | flops 35651584 | bytes 2363392 | tf_op jit(solution)/shard_map/while/body/eval_jaxpr/fh,isf->hsi/dot_general | solution.py:306
  22.3 1.3 %convolution_bitcast_fusion.2 = f32[33,8192]{1,0:T(8,128)S(1)} fusion(bf16[128,8192]{0,1:T(8,128)(2,1)S(1)} %bitcast.69, bf16[128,33]{0,1:T(8,128)(2,1)S(1)} %get-tuple-element.247), kind=kOutput, calls=%fused_computation.2.clone.1 | convolution fusion | flops 69206016 | bytes 3186944 | tf_op jit(solution)/shard_map/while/body/eval_jaxpr/ho,hn->on/dot_general | solution.py:312
  23.7 0.6 %copy.23 = f32[4,8,16,512]{3,2,1,0:T(8,128)S(1)} copy(f32[4,8,16,512]{3,1,2,0:T(8,128)S(1)} %bitcast.70) | data formatting | bytes 2097152 | tf_op jit(solution)/shard_map/while
  25.0 2.0 %gather_fusion.1 = bf16[512,256]{1,0:T(8,128)(2,1)S(1)} fusion(bf16[1024,256]{1,0:T(8,128)(2,1)S(1)} %get-tuple-element.245, s32[1024]{0:T(1024)S(1)} %pad_clamp_fusion.5), kind=kCustom, calls=%fused_computation.clone.clone.1 | custom fusion | bytes 526336 | tf_op jit(solution)/shard_map/while/body/eval_jaxpr/jit(_take)/gather | solution.py:296
  27.2 2.0 %gather_fusion = bf16[512,256]{1,0:T(8,128)(2,1)S(1)} fusion(bf16[1024,256]{1,0:T(8,128)(2,1)S(1)} %get-tuple-element.245, s32[1024]{0:T(1024)S(1)} %pad_clamp_fusion.4), kind=kCustom, calls=%fused_computation.1.clone.clone.1 | custom fusion | bytes 526336 | tf_op jit(solution)/shard_map/while/body/eval_jaxpr/jit(_take)/gather | solution.py:296
  29.3 0.3 fusion.33
  29.6 0.3 fusion.34
  29.9 0.3 slice.82
  30.1 0.3 pad_select_fusion.4
  30.4 0.3 slice.83
  30.7 0.3 pad_select_fusion.5
  31.3 0.8 %maximum_convert_fusion.2 = bf16[512,16,128]{2,0,1:T(8,128)(2,1)S(1)} fusion(bf16[512,16,16]{0,2,1:T(8,128)(2,1)S(1)} %bitcast.71, bf16[16,128]{1,0:T(8,128)(2,1)S(1)} %get-tuple-element.246), kind=kOutput, calls=%fused_computation.3.clone.1 | convolution fusion | flops 35651584 | bytes 2363392 | tf_op jit(solution)/shard_map/while/body/eval_jaxpr/fh,isf->hsi/dot_general | solution.py:306
  32.1 1.3 %convolution_bitcast_fusion.2 = f32[33,8192]{1,0:T(8,128)S(1)} fusion(bf16[128,8192]{0,1:T(8,128)(2,1)S(1)} %bitcast.69, bf16[128,33]{0,1:T(8,128)(2,1)S(1)} %get-tuple-element.247), kind=kOutput, calls=%fused_computation.2.clone.1 | convolution fusion | flops 69206016 | bytes 3186944 | tf_op jit(solution)/shard_map/while/body/eval_jaxpr/ho,hn->on/dot_general | solution.py:312
  33.5 0.6 %copy.23 = f32[4,8,16,512]{3,2,1,0:T(8,128)S(1)} copy(f32[4,8,16,512]{3,1,2,0:T(8,128)S(1)} %bitcast.70) | data formatting | bytes 2097152 | tf_op jit(solution)/shard_map/while
  34.8 18.1 %composite_head.1 = bf16[16,16,128]{2,1,0:T(8,128)(2,1)S(1)} custom-call(f32[4]{0:T(128)S(1)} %fusion.14.ahead_ref, f32[32,1024]{1,0:T(8,128)S(1)} %bitcast.65, f32[1,1024]{1,0:T(1,128)S(1)} %bitcast.68, bf16[9,32,128]{2,1,0:T(8,128)(2,1)S(1)} %copy-done.2, bf16[3,384,128]{2,1,0:T(8,128)(2,1)S(1)} %bitcast.66, bf16[3,384,128]{2,1,0:T(8,128)(2,1)S(1)} %bitcast.67), custom_call_target="tpu_custom_call" | custom-call | tf_op jit(solution)/shard_map/composite_head/pallas_call | solution.py:230
  52.9 0.6 %copy.36 = bf16[16,16,128]{2,1,0:T(8,128)(2,1)} copy(bf16[16,16,128]{2,1,0:T(8,128)(2,1)S(1)} %composite_head.1) | data formatting | bytes 131072
  (57 shorter events, 2.9 us)
Async XLA Ops:
  11.2 3.9 %copy-start.3 = (bf16[128,33]{0,1:T(8,128)(2,1)S(1)}, bf16[128,33]{0,1:T(8,128)(2,1)}, u32[]{:S(2)}) copy-start(bf16[128,33]{0,1:T(8,128)(2,1)} %param.18) | copy-start | bytes 25348
  11.2 3.9 %copy-start.4 = (bf16[16,128]{1,0:T(8,128)(2,1)S(1)}, bf16[16,128]{1,0:T(8,128)(2,1)}, u32[]{:S(2)}) copy-start(bf16[16,128]{1,0:T(8,128)(2,1)} %param.17) | copy-start | bytes 12292
  15.1 19.6 %copy-start = (bf16[9,128,128]{2,1,0:T(8,128)(2,1)S(1)}, bf16[9,128,128]{2,1,0:T(8,128)(2,1)}, u32[]{:S(2)}) copy-start(bf16[9,128,128]{2,1,0:T(8,128)(2,1)} %param.20) | copy-start | bytes 884740
  15.1 19.6 %copy-start.1 = (bf16[9,128,128]{2,1,0:T(8,128)(2,1)S(1)}, bf16[9,128,128]{2,1,0:T(8,128)(2,1)}, u32[]{:S(2)}) copy-start(bf16[9,128,128]{2,1,0:T(8,128)(2,1)} %param.21) | copy-start | bytes 884740
  15.2 19.6 %copy-start.2 = (bf16[9,32,128]{2,1,0:T(8,128)(2,1)S(1)}, bf16[9,32,128]{2,1,0:T(8,128)(2,1)}, u32[]{:S(2)}) copy-start(bf16[9,32,128]{2,1,0:T(8,128)(2,1)} %conv_in_ref.1) | copy-start | bytes 221188

commit v2 on v1

--- a/solution.py
+++ b/solution.py
@@ -1,5 +1,4 @@
 import functools
-import math
 
 import jax
 import jax.numpy as jnp
@@ -17,22 +16,113 @@
 MESH = pl.DeviceIdType.MESH
 
 
-def blend_sample_values(field, counts, bricks):
-    step_len = 8.0 / (SAMPLES * bricks)
-    slot_ids = jnp.arange(SAMPLES, dtype=jnp.int32)
-    valid = (slot_ids[:, None] < counts[None, :]).astype(jnp.float32)
-    optical = step_len * jax.nn.softplus(field[0]) * valid
-    earlier = (slot_ids[:, None] > slot_ids[None, :]).astype(jnp.float32)
-    before = jnp.dot(earlier, optical, precision=lax.Precision.HIGHEST)
-    weights = jnp.exp(-before) * (1.0 - jnp.exp(-optical))
-    colour = jnp.sum(weights[None] * field[1:], axis=1)
-    return (colour, jnp.sum(optical, axis=0))
+def march_kernel(
+    step_len,
+    entries_ref,
+    counts_ref,
+    features_ref,
+    first_ref,
+    second_ref,
+    colour_ref,
+    depth_ref,
+    table,
+    windows,
+):
+    channels = colour_ref.shape[0]
+    rays = colour_ref.shape[1]
+    cells = table.shape[0]
+    lanes = table.shape[1]
+    chunk = 1024
+    wide = second_ref[...].astype(jnp.float32)
+    wide = jnp.concatenate(
+        [
+            wide[:, 1:],
+            jnp.broadcast_to(wide[:, :1], (wide.shape[0], lanes - channels)),
+        ],
+        axis=1,
+    ).astype(jnp.bfloat16)
+    lane = lax.broadcasted_iota(jnp.int32, (1, lanes), 1)
+
+    def fill(step, carry):
+        start = pl.multiple_of(step * chunk, chunk)
+        block = features_ref[:, 0, 0, pl.ds(start, chunk)]
+        hidden = lax.dot_general(
+            block, first_ref[...], (((0,), (0,)), ((), ())), preferred_element_type=jnp.float32
+        )
+        hidden = jnp.maximum(hidden, 0.0).astype(jnp.bfloat16)
+        field = jnp.dot(hidden, wide, preferred_element_type=jnp.float32)
+        optical = step_len * (jnp.maximum(field, 0.0) + jnp.log1p(jnp.exp(-jnp.abs(field))))
+        through = jnp.exp(-optical)
+        stopped = pltpu.roll(1.0 - through, lanes - channels, 1)
+        table[pl.ds(start, chunk), :] = jnp.where(
+            lane < channels,
+            stopped * field,
+            jnp.where(lane < 2 * channels, through, optical),
+        )
+        return carry
+
+    lax.fori_loop(0, cells // chunk, fill, 0)
+    block_rays = windows.shape[0] // SAMPLES
+    slot = lax.broadcasted_iota(jnp.int32, (SAMPLES, lanes), 0)
+
+    def blend(step, carry):
+        base = step * block_rays
+
+        def fetch(ray, inner):
+            window = table[pl.ds(entries_ref[0, 0, base + ray], SAMPLES), :]
+            window = jnp.where(slot < counts_ref[0, 0, base + ray], window, 0.0)
+            windows[pl.ds(ray, SAMPLES, stride=block_rays), :] = window
+            return inner
+
+        lax.fori_loop(0, block_rays, fetch, 0, unroll=16)
+        total = windows[:block_rays, :]
+        scale = jnp.ones_like(total)
+        previous = total
+        for index in range(1, SAMPLES):
+            scale = scale * jnp.where(
+                lane < channels, pltpu.roll(previous, lanes - channels, 1), 1.0
+            )
+            previous = windows[index * block_rays : (index + 1) * block_rays, :]
+            total = total + scale * previous
+        turned = jnp.transpose(total)
+        place = pl.ds(pl.multiple_of(base, block_rays), block_rays)
+        colour_ref[:, place] = turned[:channels]
+        depth_ref[:, place] = turned[2 * channels : 2 * channels + 1]
+        return carry
+
+    lax.fori_loop(0, rays // block_rays, blend, 0)
+
+
+def march(entries, counts, features, first_weight, second_weight):
+    rays = entries.shape[2]
+    cells = features.shape[3]
+    channels = second_weight.shape[1] - 1
+    lanes = 4 * channels
+    block_rays = 128
+    smem = pl.BlockSpec(memory_space=pltpu.SMEM)
+    vmem = pl.BlockSpec(memory_space=pltpu.VMEM)
+    step_len = 8.0 / (SAMPLES * lax.axis_size("depth"))
+    return pl.pallas_call(
+        functools.partial(march_kernel, step_len),
+        out_shape=(
+            jax.ShapeDtypeStruct((channels, rays), jnp.float32),
+            jax.ShapeDtypeStruct((1, rays), jnp.float32),
+        ),
+        in_specs=[smem, smem, vmem, vmem, vmem],
+        out_specs=(vmem, vmem),
+        scratch_shapes=[
+            pltpu.VMEM((cells, lanes), jnp.float32),
+            pltpu.VMEM((SAMPLES * block_rays, lanes), jnp.float32),
+        ],
+        compiler_params=pltpu.CompilerParams(vmem_limit_bytes=48 * 1024 * 1024),
+        name="march",
+    )(entries, counts, features, first_weight, second_weight)
 
 
 def composite_head(
     bricks,
     tiles,
-    ahead_ref,
+    rank_ref,
     colour_ref,
     depth_ref,
     conv_in_ref,
@@ -93,7 +183,8 @@
         depth_copy(peer, peer).wait_recv()
     front = jnp.zeros_like(depth_ref)
     for brick in range(bricks):
-        front = front + ahead_ref[brick] * depths[brick]
+        nearer = jnp.where(rank_ref[0, brick] < rank_ref[0, me], 1.0, 0.0)
+        front = front + nearer * depths[brick]
     dimmed = (colour_ref[...] * jnp.exp(-front)).astype(jnp.bfloat16).astype(jnp.float32)
     margin = jnp.zeros((channels, HALO * COLS_DEV), jnp.float32)
     outbox[...] = jnp.concatenate([margin, dimmed, margin], axis=1).astype(jnp.bfloat16)
@@ -220,7 +311,7 @@
         side_copy(1).wait_send()
 
 
-def composite(ahead, colour, depth_sum, conv_in, conv_mid, conv_out):
+def composite(ranks, colour, depth_sum, conv_in, conv_mid, conv_out):
     bricks = lax.axis_size("depth")
     tiles = lax.axis_size("rays")
     channels, rays = colour.shape
@@ -250,7 +341,7 @@
         ),
         name="composite_head",
     )(
-        ahead,
+        ranks,
         colour,
         depth_sum,
         conv_in,
@@ -270,56 +361,10 @@
     conv_mid,
     conv_out,
 ):
-    bricks = lax.axis_size("depth")
-    feat_count = brick_features.shape[0]
-    cell_count = brick_features.shape[3]
-    windows = cell_count // SAMPLES
-    span = SAMPLES * feat_count
-    table = (
-        brick_features.reshape(feat_count, windows, SAMPLES)
-        .transpose(1, 2, 0)
-        .reshape(windows, span)
+    colour, depth_sum = march(
+        entry_cells, sample_counts, brick_features, input_layer_weight, second_weight
     )
-    entries = entry_cells.reshape(-1)
-    counts = sample_counts.reshape(-1)
-    ranks = brick_rank.reshape(-1)
-    total_rays = entries.shape[0]
-    block = math.gcd(total_rays, 512)
-    shift_bits = (SAMPLES - 1).bit_length()
-
-    def march_block(operands):
-        block_entries, block_counts = operands
-        window_ids = block_entries // SAMPLES
-        offset = block_entries - window_ids * SAMPLES
-        following = jnp.minimum(window_ids + 1, windows - 1)
-        paired = jnp.concatenate(
-            [jnp.take(table, window_ids, axis=0), jnp.take(table, following, axis=0)], axis=1
-        )
-        for level in range(shift_bits):
-            moved_by = (1 << level) * feat_count
-            moved = jnp.concatenate(
-                [paired[:, moved_by:], jnp.zeros((block, moved_by), paired.dtype)], axis=1
-            )
-            taken = (offset >> level & 1)[:, None] == 1
-            paired = jnp.where(taken, moved, paired)
-        probed_values = paired[:, :span].reshape(block, SAMPLES, feat_count)
-        before_activation = jnp.einsum(
-            "fh,isf->hsi", input_layer_weight, probed_values, preferred_element_type=jnp.float32
-        )
-        hidden = (
-            jnp.maximum(before_activation, 0.0).astype(jnp.bfloat16).reshape(-1, SAMPLES * block)
-        )
-        field = jnp.einsum("ho,hn->on", second_weight, hidden, preferred_element_type=jnp.float32)
-        return blend_sample_values(field.reshape(-1, SAMPLES, block), block_counts, bricks)
-
-    colour_blocks, depth_blocks = lax.map(
-        march_block, (entries.reshape(-1, block), counts.reshape(-1, block))
-    )
-    colour = jnp.transpose(colour_blocks, (1, 0, 2)).reshape(colour_blocks.shape[1], total_rays)
-    depth_sum = depth_blocks.reshape(1, total_rays)
-    my_rank = ranks[lax.axis_index("depth")]
-    ahead = (ranks < my_rank).astype(jnp.float32)
-    return composite(ahead, colour, depth_sum, conv_in, conv_mid, conv_out)
+    return composite(brick_rank, colour, depth_sum, conv_in, conv_mid, conv_out)
 
 
 def solution(mesh):

time: 53.9 us -> 47 us (0.87)
  Pallas kernels: 18.1 us -> 42.5 us
  local copies, waits for them, and re-layouts: 22.7 us -> 4.19 us
  other arithmetic: 7.7 us -> 0 us
  matrix products: 4.49 us -> 0 us
    pallas_call x0 -> x1, Pallas kernels: none -> 24.4 us  [march(): pl.pallas_call(functools.partial(march_kernel, step_len), out_shape=(jax....]
    gather x4 -> x0, local copies, waits for them, and re-layouts: 7.81 us -> none  [the longest x2 3.91 us: march_block(): jnp.take(table, window_ids, axis=0)]
    reshape x2 -> x0, local copies, waits for them, and re-layouts: 5.43 us -> none  [the longest x1 5.42 us: shards(): brick_features.reshape(feat_count, windows, SAMPLES).transpose(1, 2, 0)]
    dot_general x6 -> x0, matrix products: 4.49 us -> none  [the longest x2 2.63 us: march_block(): jnp.einsum('ho,hn->on', second_weight, hidden, preferred_element_type=jnp...]
    transpose x1 -> x0, local copies, waits for them, and re-layouts: 3.68 us -> none  [shards(): table = brick_features.reshape(feat_count, windows, SAMPLES).transpose(1,...]
    unnamed x13 -> x17, local copies, waits for them, and re-layouts: 1.17 us -> 4.19 us
    unnamed x2 -> x0, other arithmetic: 2.69 us -> none
    select_n x14 -> x0, other arithmetic: 2.43 us -> none  [the longest x8 1.87 us: march_block(): paired = jnp.where(taken, moved, paired)]
where the time goes in v2:
time: 47 us; the launch traced here: 46.8 us
  Pallas kernels  42.5 us (90%)
  local copies, waits for them, and re-layouts  4.19 us (9%)
    pallas_call x1, Pallas kernels, march(): pl.pallas_call(functools.partial(march_kernel, step_len), out_shape=(jax....  24.4 us
    pallas_call x1, Pallas kernels, composite(): pl.pallas_call(functools.partial(composite_head, bricks, tiles), out_shap...  18.1 us
    unnamed x17, local copies, waits for them, and re-layouts  4.19 us

profile of v2, /device:TPU:1, one launch (start us, length us, event | category | flops | bytes accessed | tf_op | source)
XLA Modules:
  0.0 46.8 jit_solution(16595629225924128725)
XLA Ops:
  0.0 0.8 %copy.11.second_ref = bf16[128,33]{1,0:T(8,128)(2,1)S(1)} copy(bf16[128,33]{0,1:T(8,128)(2,1)} %param.14) | data formatting | bytes 16896 | tf_op args[5]
  0.8 0.0 copy-start.3
  0.8 0.0 copy-start.4
  0.8 0.0 copy-start.5
  0.9 2.1 %copy.10.features_ref = bf16[16,1,1,16384]{3,2,1,0:T(2,128)(2,1)S(1)} copy(bf16[16,1,1,16384]{3,0,2,1:T(8,128)(2,1)} %param.9) | data formatting | bytes 1048576 | tf_op args[0]
  2.9 0.0 copy-done.3
  2.9 0.0 copy-done.4
  2.9 0.0 copy-done.5
  3.0 0.0 copy-start
  3.0 0.0 copy-start.1
  3.0 0.0 copy-start.2
  3.0 24.4 %march.1 = (f32[32,1024]{1,0:T(8,128)S(1)}, f32[1,1024]{1,0:T(1,128)S(1)}) custom-call(s32[1,1,1024]{2,1,0:T(1,128)S(1)} %copy-done.3, s32[1,1,1024]{2,1,0:T(1,128)S(1)} %copy-done.4, bf16[16,1,1,16384]{3,2,1,0:T(2,128)(2,1)S(1)} %copy.10.features_ref, bf16[16,128]{1,0:T(8,128)(2,1)S(1)} %copy-done.5, bf16[128,33]{1,0:T(8,128)(2,1)S(1)} %copy.11.second_ref), custom_call_target="tpu_custom_call" | custom-call | tf_op jit(solution)/shard_map/march/pallas_call | solution.py:105
  27.4 0.0 copy-start.6
  27.4 0.0 copy-done
  27.4 0.0 copy-done.1
  27.4 0.0 copy-done.2
  27.4 0.6 %copy-done.6 = s32[1,4]{1,0:T(1,128)S(1)} copy-done((s32[1,4]{1,0:T(1,128)S(1)}, s32[1,4]{1,0:T(1,128)}, u32[]{:S(2)}) %copy-start.6) | copy-done | bytes 40
  28.1 18.1 %composite_head.1 = bf16[16,16,128]{2,1,0:T(8,128)(2,1)S(1)} custom-call(s32[1,4]{1,0:T(1,128)S(1)} %copy-done.6, f32[32,1024]{1,0:T(8,128)S(1)} %get-tuple-element.7.colour_ref, f32[1,1024]{1,0:T(1,128)S(1)} %get-tuple-element.8.depth_ref, bf16[9,32,128]{2,1,0:T(8,128)(2,1)S(1)} %copy-done.2, bf16[3,384,128]{2,1,0:T(8,128)(2,1)S(1)} %bitcast.2, ...), custom_call_target="tpu_custom_call" | custom-call | tf_op jit(solution)/shard_map/composite_head/pallas_call | solution.py:321
  46.2 0.6 %copy.13 = bf16[16,16,128]{2,1,0:T(8,128)(2,1)} copy(bf16[16,16,128]{2,1,0:T(8,128)(2,1)S(1)} %composite_head.1) | data formatting | bytes 131072
Async XLA Ops:
  0.8 2.1 %copy-start.3 = (s32[1,1,1024]{2,1,0:T(1,128)S(1)}, s32[1,1,1024]{2,1,0:T(1,128)}, u32[]{:S(2)}) copy-start(s32[1,1,1024]{2,1,0:T(1,128)} %entries_ref.1) | copy-start | bytes 12292
  0.8 2.1 %copy-start.4 = (s32[1,1,1024]{2,1,0:T(1,128)S(1)}, s32[1,1,1024]{2,1,0:T(1,128)}, u32[]{:S(2)}) copy-start(s32[1,1,1024]{2,1,0:T(1,128)} %counts_ref.1) | copy-start | bytes 12292
  0.8 2.1 %copy-start.5 = (bf16[16,128]{1,0:T(8,128)(2,1)S(1)}, bf16[16,128]{1,0:T(8,128)(2,1)}, u32[]{:S(2)}) copy-start(bf16[16,128]{1,0:T(8,128)(2,1)} %first_ref.1) | copy-start | bytes 12292
  3.0 24.4 %copy-start = (bf16[9,128,128]{2,1,0:T(8,128)(2,1)S(1)}, bf16[9,128,128]{2,1,0:T(8,128)(2,1)}, u32[]{:S(2)}) copy-start(bf16[9,128,128]{2,1,0:T(8,128)(2,1)} %param.16) | copy-start | bytes 884740
  3.0 24.4 %copy-start.1 = (bf16[9,128,128]{2,1,0:T(8,128)(2,1)S(1)}, bf16[9,128,128]{2,1,0:T(8,128)(2,1)}, u32[]{:S(2)}) copy-start(bf16[9,128,128]{2,1,0:T(8,128)(2,1)} %param.17) | copy-start | bytes 884740
  3.0 24.4 %copy-start.2 = (bf16[9,32,128]{2,1,0:T(8,128)(2,1)S(1)}, bf16[9,32,128]{2,1,0:T(8,128)(2,1)}, u32[]{:S(2)}) copy-start(bf16[9,32,128]{2,1,0:T(8,128)(2,1)} %conv_in_ref.1) | copy-start | bytes 221188
  27.4 0.7 %copy-start.6 = (s32[1,4]{1,0:T(1,128)S(1)}, s32[1,4]{1,0:T(1,128)}, u32[]{:S(2)}) copy-start(s32[1,4]{1,0:T(1,128)} %rank_ref.1) | copy-start | bytes 52

commit v3 on v2

--- a/solution.py
+++ b/solution.py
@@ -41,28 +41,34 @@
         ],
         axis=1,
     ).astype(jnp.bfloat16)
+    turned_weight = jnp.transpose(wide.astype(jnp.float32))[: channels + 8].astype(jnp.bfloat16)
     lane = lax.broadcasted_iota(jnp.int32, (1, lanes), 1)
 
     def fill(step, carry):
         start = pl.multiple_of(step * chunk, chunk)
         block = features_ref[:, 0, 0, pl.ds(start, chunk)]
         hidden = lax.dot_general(
-            block, first_ref[...], (((0,), (0,)), ((), ())), preferred_element_type=jnp.float32
+            first_ref[...], block, (((0,), (0,)), ((), ())), preferred_element_type=jnp.float32
         )
         hidden = jnp.maximum(hidden, 0.0).astype(jnp.bfloat16)
-        field = jnp.dot(hidden, wide, preferred_element_type=jnp.float32)
-        optical = step_len * (jnp.maximum(field, 0.0) + jnp.log1p(jnp.exp(-jnp.abs(field))))
+        field = jnp.dot(turned_weight, hidden, preferred_element_type=jnp.float32)
+        logit = field[channels : channels + 1]
+        optical = step_len * (jnp.maximum(logit, 0.0) + jnp.log1p(jnp.exp(-jnp.abs(logit))))
         through = jnp.exp(-optical)
-        stopped = pltpu.roll(1.0 - through, lanes - channels, 1)
-        table[pl.ds(start, chunk), :] = jnp.where(
-            lane < channels,
-            stopped * field,
-            jnp.where(lane < 2 * channels, through, optical),
-        )
+        joined = jnp.concatenate(
+            [
+                (1.0 - through) * field[:channels],
+                jnp.broadcast_to(through, (channels, chunk)),
+                jnp.broadcast_to(optical, (lanes - 2 * channels, chunk)),
+            ],
+            axis=0,
+        )
+        table[pl.ds(start, chunk), :] = jnp.transpose(joined)
         return carry
 
-    lax.fori_loop(0, cells // chunk, fill, 0)
-    block_rays = windows.shape[0] // SAMPLES
+    lax.fori_loop(0, cells // chunk, fill, 0, unroll=4)
+    pitch = windows.shape[0] // SAMPLES
+    block_rays = pitch - 8
     slot = lax.broadcasted_iota(jnp.int32, (SAMPLES, lanes), 0)
 
     def blend(step, carry):
@@ -71,7 +77,7 @@
         def fetch(ray, inner):
             window = table[pl.ds(entries_ref[0, 0, base + ray], SAMPLES), :]
             window = jnp.where(slot < counts_ref[0, 0, base + ray], window, 0.0)
-            windows[pl.ds(ray, SAMPLES, stride=block_rays), :] = window
+            windows[pl.ds(ray, SAMPLES, stride=pitch), :] = window
             return inner
 
         lax.fori_loop(0, block_rays, fetch, 0, unroll=16)
@@ -82,7 +88,7 @@
             scale = scale * jnp.where(
                 lane < channels, pltpu.roll(previous, lanes - channels, 1), 1.0
             )
-            previous = windows[index * block_rays : (index + 1) * block_rays, :]
+            previous = windows[index * pitch : index * pitch + block_rays, :]
             total = total + scale * previous
         turned = jnp.transpose(total)
         place = pl.ds(pl.multiple_of(base, block_rays), block_rays)
@@ -112,7 +118,7 @@
         out_specs=(vmem, vmem),
         scratch_shapes=[
             pltpu.VMEM((cells, lanes), jnp.float32),
-            pltpu.VMEM((SAMPLES * block_rays, lanes), jnp.float32),
+            pltpu.VMEM((SAMPLES * (block_rays + 8), lanes), jnp.float32),
         ],
         compiler_params=pltpu.CompilerParams(vmem_limit_bytes=48 * 1024 * 1024),
         name="march",

time: 47 us -> 34.2 us (0.73)
  Pallas kernels: 42.5 us -> 29.7 us
    pallas_call x1, Pallas kernels: 24.4 us -> 11.6 us  [march(): pl.pallas_call(functools.partial(march_kernel, step_len), out_shape=(jax....]
where the time goes in v3:
time: 34.2 us; the launch traced here: 34 us
  Pallas kernels  29.7 us (87%)
  local copies, waits for them, and re-layouts  4.19 us (12%)
    pallas_call x1, Pallas kernels, composite(): pl.pallas_call(functools.partial(composite_head, bricks, tiles), out_shap...  18.1 us
    pallas_call x1, Pallas kernels, march(): pl.pallas_call(functools.partial(march_kernel, step_len), out_shape=(jax....  11.6 us
    unnamed x17, local copies, waits for them, and re-layouts  4.19 us

profile of v3, /device:TPU:1, one launch (start us, length us, event | category | flops | bytes accessed | tf_op | source)
XLA Modules:
  0.0 34.0 jit_solution(13059447207522940506)
XLA Ops:
  0.0 0.8 %copy.11.second_ref = bf16[128,33]{1,0:T(8,128)(2,1)S(1)} copy(bf16[128,33]{0,1:T(8,128)(2,1)} %param.14) | data formatting | bytes 16896 | tf_op args[5]
  0.8 0.0 copy-start.3
  0.8 0.0 copy-start.4
  0.8 0.0 copy-start.5
  0.9 2.1 %copy.10.features_ref = bf16[16,1,1,16384]{3,2,1,0:T(2,128)(2,1)S(1)} copy(bf16[16,1,1,16384]{3,0,2,1:T(8,128)(2,1)} %param.9) | data formatting | bytes 1048576 | tf_op args[0]
  2.9 0.0 copy-done.3
  2.9 0.0 copy-done.4
  2.9 0.0 copy-done.5
  3.0 0.0 copy-start
  3.0 0.0 copy-start.1
  3.0 0.0 copy-start.2
  3.0 11.6 %march.1 = (f32[32,1024]{1,0:T(8,128)S(1)}, f32[1,1024]{1,0:T(1,128)S(1)}) custom-call(s32[1,1,1024]{2,1,0:T(1,128)S(1)} %copy-done.3, s32[1,1,1024]{2,1,0:T(1,128)S(1)} %copy-done.4, bf16[16,1,1,16384]{3,2,1,0:T(2,128)(2,1)S(1)} %copy.10.features_ref, bf16[16,128]{1,0:T(8,128)(2,1)S(1)} %copy-done.5, bf16[128,33]{1,0:T(8,128)(2,1)S(1)} %copy.11.second_ref), custom_call_target="tpu_custom_call" | custom-call | tf_op jit(solution)/shard_map/march/pallas_call | solution.py:111
  14.6 0.0 copy-start.6
  14.6 0.0 copy-done
  14.6 0.0 copy-done.1
  14.6 0.0 copy-done.2
  14.6 0.6 %copy-done.6 = s32[1,4]{1,0:T(1,128)S(1)} copy-done((s32[1,4]{1,0:T(1,128)S(1)}, s32[1,4]{1,0:T(1,128)}, u32[]{:S(2)}) %copy-start.6) | copy-done | bytes 40
  15.2 18.1 %composite_head.1 = bf16[16,16,128]{2,1,0:T(8,128)(2,1)S(1)} custom-call(s32[1,4]{1,0:T(1,128)S(1)} %copy-done.6, f32[32,1024]{1,0:T(8,128)S(1)} %get-tuple-element.7.colour_ref, f32[1,1024]{1,0:T(1,128)S(1)} %get-tuple-element.8.depth_ref, bf16[9,32,128]{2,1,0:T(8,128)(2,1)S(1)} %copy-done.2, bf16[3,384,128]{2,1,0:T(8,128)(2,1)S(1)} %bitcast.2, ...), custom_call_target="tpu_custom_call" | custom-call | tf_op jit(solution)/shard_map/composite_head/pallas_call | solution.py:327
  33.4 0.6 %copy.13 = bf16[16,16,128]{2,1,0:T(8,128)(2,1)} copy(bf16[16,16,128]{2,1,0:T(8,128)(2,1)S(1)} %composite_head.1) | data formatting | bytes 131072
Async XLA Ops:
  0.8 2.1 %copy-start.3 = (s32[1,1,1024]{2,1,0:T(1,128)S(1)}, s32[1,1,1024]{2,1,0:T(1,128)}, u32[]{:S(2)}) copy-start(s32[1,1,1024]{2,1,0:T(1,128)} %entries_ref.1) | copy-start | bytes 12292
  0.8 2.1 %copy-start.4 = (s32[1,1,1024]{2,1,0:T(1,128)S(1)}, s32[1,1,1024]{2,1,0:T(1,128)}, u32[]{:S(2)}) copy-start(s32[1,1,1024]{2,1,0:T(1,128)} %counts_ref.1) | copy-start | bytes 12292
  0.8 2.1 %copy-start.5 = (bf16[16,128]{1,0:T(8,128)(2,1)S(1)}, bf16[16,128]{1,0:T(8,128)(2,1)}, u32[]{:S(2)}) copy-start(bf16[16,128]{1,0:T(8,128)(2,1)} %first_ref.1) | copy-start | bytes 12292
  3.0 11.6 %copy-start = (bf16[9,128,128]{2,1,0:T(8,128)(2,1)S(1)}, bf16[9,128,128]{2,1,0:T(8,128)(2,1)}, u32[]{:S(2)}) copy-start(bf16[9,128,128]{2,1,0:T(8,128)(2,1)} %param.16) | copy-start | bytes 884740
  3.0 11.6 %copy-start.1 = (bf16[9,128,128]{2,1,0:T(8,128)(2,1)S(1)}, bf16[9,128,128]{2,1,0:T(8,128)(2,1)}, u32[]{:S(2)}) copy-start(bf16[9,128,128]{2,1,0:T(8,128)(2,1)} %param.17) | copy-start | bytes 884740
  3.0 11.6 %copy-start.2 = (bf16[9,32,128]{2,1,0:T(8,128)(2,1)S(1)}, bf16[9,32,128]{2,1,0:T(8,128)(2,1)}, u32[]{:S(2)}) copy-start(bf16[9,32,128]{2,1,0:T(8,128)(2,1)} %conv_in_ref.1) | copy-start | bytes 221188
  14.6 0.7 %copy-start.6 = (s32[1,4]{1,0:T(1,128)S(1)}, s32[1,4]{1,0:T(1,128)}, u32[]{:S(2)}) copy-start(s32[1,4]{1,0:T(1,128)} %rank_ref.1) | copy-start | bytes 52

commit v4 on v3

--- a/solution.py
+++ b/solution.py
@@ -33,20 +33,15 @@
     cells = table.shape[0]
     lanes = table.shape[1]
     chunk = 1024
-    wide = second_ref[...].astype(jnp.float32)
-    wide = jnp.concatenate(
-        [
-            wide[:, 1:],
-            jnp.broadcast_to(wide[:, :1], (wide.shape[0], lanes - channels)),
-        ],
-        axis=1,
+    turned = second_ref[...].astype(jnp.float32)
+    turned_weight = jnp.concatenate(
+        [turned[1:], jnp.broadcast_to(turned[:1], (8, turned.shape[1]))], axis=0
     ).astype(jnp.bfloat16)
-    turned_weight = jnp.transpose(wide.astype(jnp.float32))[: channels + 8].astype(jnp.bfloat16)
     lane = lax.broadcasted_iota(jnp.int32, (1, lanes), 1)
 
     def fill(step, carry):
         start = pl.multiple_of(step * chunk, chunk)
-        block = features_ref[:, 0, 0, pl.ds(start, chunk)]
+        block = features_ref[0, 0, :, pl.ds(start, chunk)]
         hidden = lax.dot_general(
             first_ref[...], block, (((0,), (0,)), ((), ())), preferred_element_type=jnp.float32
         )
@@ -122,7 +117,7 @@
         ],
         compiler_params=pltpu.CompilerParams(vmem_limit_bytes=48 * 1024 * 1024),
         name="march",
-    )(entries, counts, features, first_weight, second_weight)
+    )(entries, counts, features.transpose(1, 2, 0, 3), first_weight, second_weight.T)
 
 
 def composite_head(

time: 34.2 us -> 35.8 us (1.047)
  local copies, waits for them, and re-layouts: 4.19 us -> 6.04 us
    unnamed x17 -> x19, local copies, waits for them, and re-layouts: 4.19 us -> 6.04 us
where the time goes in v4:
time: 35.8 us; the launch traced here: 35.5 us
  Pallas kernels  29.4 us (82%)
  local copies, waits for them, and re-layouts  6.04 us (17%)
    pallas_call x1, Pallas kernels, composite(): pl.pallas_call(functools.partial(composite_head, bricks, tiles), out_shap...  18.1 us
    pallas_call x1, Pallas kernels, march(): pl.pallas_call(functools.partial(march_kernel, step_len), out_shape=(jax....  11.3 us
    unnamed x19, local copies, waits for them, and re-layouts  6.04 us

profile of v4, /device:TPU:1, one launch (start us, length us, event | category | flops | bytes accessed | tf_op | source)
XLA Modules:
  0.0 35.5 jit_solution(825666032422970159)
XLA Ops:
  0.0 0.0 copy-start.5
  0.0 0.7 %copy-done.5 = s32[1,1,1024]{2,1,0:T(1,128)S(1)} copy-done((s32[1,1,1024]{2,1,0:T(1,128)S(1)}, s32[1,1,1024]{2,1,0:T(1,128)}, u32[]{:S(2)}) %copy-start.5) | copy-done | bytes 4120
  0.7 0.0 copy-start
  0.7 1.0 %copy-done = bf16[16,1,1,16384]{3,0,2,1:T(8,128)(2,1)S(1)} copy-done((bf16[16,1,1,16384]{3,0,2,1:T(8,128)(2,1)S(1)}, bf16[16,1,1,16384]{3,0,2,1:T(8,128)(2,1)}, u32[]{:S(2)}) %copy-start) | copy-done | bytes 524312
  1.7 0.0 copy-start.4
  1.7 0.7 %copy-done.4 = bf16[128,33]{0,1:T(8,128)(2,1)S(1)} copy-done((bf16[128,33]{0,1:T(8,128)(2,1)S(1)}, bf16[128,33]{0,1:T(8,128)(2,1)}, u32[]{:S(2)}) %copy-start.4) | copy-done | bytes 8472
  2.4 0.0 copy-start.6
  2.4 0.7 %copy-done.6 = s32[1,1,1024]{2,1,0:T(1,128)S(1)} copy-done((s32[1,1,1024]{2,1,0:T(1,128)S(1)}, s32[1,1,1024]{2,1,0:T(1,128)}, u32[]{:S(2)}) %copy-start.6) | copy-done | bytes 4120
  3.1 0.0 copy-start.7
  3.1 0.7 %copy-done.7 = bf16[16,128]{1,0:T(8,128)(2,1)S(1)} copy-done((bf16[16,128]{1,0:T(8,128)(2,1)S(1)}, bf16[16,128]{1,0:T(8,128)(2,1)}, u32[]{:S(2)}) %copy-start.7) | copy-done | bytes 4120
  3.8 0.0 copy-start.1
  3.8 0.0 copy-start.3
  3.8 11.3 %march.1 = (f32[32,1024]{1,0:T(8,128)S(1)}, f32[1,1024]{1,0:T(1,128)S(1)}) custom-call(s32[1,1,1024]{2,1,0:T(1,128)S(1)} %copy-done.5, s32[1,1,1024]{2,1,0:T(1,128)S(1)} %copy-done.6, bf16[1,1,16,16384]{3,2,1,0:T(8,128)(2,1)S(1)} %bitcast.4, bf16[16,128]{1,0:T(8,128)(2,1)S(1)} %copy-done.7, bf16[33,128]{1,0:T(8,128)(2,1)S(1)} %bitcast.7), custom_call_target="tpu_custom_call" | custom-call | tf_op jit(solution)/shard_map/march/pallas_call | solution.py:106
  15.1 0.0 copy-start.8
  15.1 0.0 copy-done.1
  15.1 0.0 copy-done.3
  15.1 0.6 %copy-done.8 = s32[1,4]{1,0:T(1,128)S(1)} copy-done((s32[1,4]{1,0:T(1,128)S(1)}, s32[1,4]{1,0:T(1,128)}, u32[]{:S(2)}) %copy-start.8) | copy-done | bytes 40
  15.8 0.0 copy-start.2
  15.8 1.0 %copy-done.2 = bf16[9,128,128]{2,1,0:T(8,128)(2,1)S(1)} copy-done((bf16[9,128,128]{2,1,0:T(8,128)(2,1)S(1)}, bf16[9,128,128]{2,1,0:T(8,128)(2,1)}, u32[]{:S(2)}) %copy-start.2) | copy-done | bytes 294936
  16.7 18.1 %composite_head.1 = bf16[16,16,128]{2,1,0:T(8,128)(2,1)S(1)} custom-call(s32[1,4]{1,0:T(1,128)S(1)} %copy-done.8, f32[32,1024]{1,0:T(8,128)S(1)} %get-tuple-element.7.colour_ref, f32[1,1024]{1,0:T(1,128)S(1)} %get-tuple-element.8.depth_ref, bf16[9,32,128]{2,1,0:T(8,128)(2,1)S(1)} %copy-done.3, bf16[3,384,128]{2,1,0:T(8,128)(2,1)S(1)} %bitcast.5, ...), custom_call_target="tpu_custom_call" | custom-call | tf_op jit(solution)/shard_map/composite_head/pallas_call | solution.py:322
  34.9 0.6 %copy.11 = bf16[16,16,128]{2,1,0:T(8,128)(2,1)} copy(bf16[16,16,128]{2,1,0:T(8,128)(2,1)S(1)} %composite_head.1) | data formatting | bytes 131072
Async XLA Ops:
  0.0 0.7 %copy-start.5 = (s32[1,1,1024]{2,1,0:T(1,128)S(1)}, s32[1,1,1024]{2,1,0:T(1,128)}, u32[]{:S(2)}) copy-start(s32[1,1,1024]{2,1,0:T(1,128)} %entries_ref.1) | copy-start | bytes 12292
  0.7 1.0 %copy-start = (bf16[16,1,1,16384]{3,0,2,1:T(8,128)(2,1)S(1)}, bf16[16,1,1,16384]{3,0,2,1:T(8,128)(2,1)}, u32[]{:S(2)}) copy-start(bf16[16,1,1,16384]{3,0,2,1:T(8,128)(2,1)} %param.9) | copy-start | bytes 1572868
  1.7 0.7 %copy-start.4 = (bf16[128,33]{0,1:T(8,128)(2,1)S(1)}, bf16[128,33]{0,1:T(8,128)(2,1)}, u32[]{:S(2)}) copy-start(bf16[128,33]{0,1:T(8,128)(2,1)} %param.14) | copy-start | bytes 25348
  2.4 0.7 %copy-start.6 = (s32[1,1,1024]{2,1,0:T(1,128)S(1)}, s32[1,1,1024]{2,1,0:T(1,128)}, u32[]{:S(2)}) copy-start(s32[1,1,1024]{2,1,0:T(1,128)} %counts_ref.1) | copy-start | bytes 12292
  3.1 0.7 %copy-start.7 = (bf16[16,128]{1,0:T(8,128)(2,1)S(1)}, bf16[16,128]{1,0:T(8,128)(2,1)}, u32[]{:S(2)}) copy-start(bf16[16,128]{1,0:T(8,128)(2,1)} %first_ref.1) | copy-start | bytes 12292
  3.8 11.3 %copy-start.1 = (bf16[9,128,128]{2,1,0:T(8,128)(2,1)S(1)}, bf16[9,128,128]{2,1,0:T(8,128)(2,1)}, u32[]{:S(2)}) copy-start(bf16[9,128,128]{2,1,0:T(8,128)(2,1)} %param.16) | copy-start | bytes 884740
  3.8 11.3 %copy-start.3 = (bf16[9,32,128]{2,1,0:T(8,128)(2,1)S(1)}, bf16[9,32,128]{2,1,0:T(8,128)(2,1)}, u32[]{:S(2)}) copy-start(bf16[9,32,128]{2,1,0:T(8,128)(2,1)} %conv_in_ref.1) | copy-start | bytes 221188
  15.1 0.7 %copy-start.8 = (s32[1,4]{1,0:T(1,128)S(1)}, s32[1,4]{1,0:T(1,128)}, u32[]{:S(2)}) copy-start(s32[1,4]{1,0:T(1,128)} %rank_ref.1) | copy-start | bytes 52
  15.8 1.0 %copy-start.2 = (bf16[9,128,128]{2,1,0:T(8,128)(2,1)S(1)}, bf16[9,128,128]{2,1,0:T(8,128)(2,1)}, u32[]{:S(2)}) copy-start(bf16[9,128,128]{2,1,0:T(8,128)(2,1)} %param.17) | copy-start | bytes 884740

commit v5 on v4

--- a/solution.py
+++ b/solution.py
@@ -115,7 +115,7 @@
             pltpu.VMEM((cells, lanes), jnp.float32),
             pltpu.VMEM((SAMPLES * (block_rays + 8), lanes), jnp.float32),
         ],
-        compiler_params=pltpu.CompilerParams(vmem_limit_bytes=48 * 1024 * 1024),
+        compiler_params=pltpu.CompilerParams(vmem_limit_bytes=63 * 1024 * 1024),
         name="march",
     )(entries, counts, features.transpose(1, 2, 0, 3), first_weight, second_weight.T)
 
@@ -338,7 +338,7 @@
             dma((2,)),
         ],
         compiler_params=pltpu.CompilerParams(
-            collective_id=0, has_side_effects=True, vmem_limit_bytes=48 * 1024 * 1024
+            collective_id=0, has_side_effects=True, vmem_limit_bytes=63 * 1024 * 1024
         ),
         name="composite_head",
     )(

time: 35.8 us -> 33.4 us (0.933)
  local copies, waits for them, and re-layouts: 6.04 us -> 1.47 us
  Pallas kernels: 29.4 us -> 31.8 us
    unnamed x19 -> x1, local copies, waits for them, and re-layouts: 6.04 us -> 1.47 us
    pallas_call x1, Pallas kernels: 18.1 us -> 19.4 us  [composite(): pl.pallas_call(functools.partial(composite_head, bricks, tiles), out_shap...]
    pallas_call x1, Pallas kernels: 11.3 us -> 12.4 us  [march(): pl.pallas_call(functools.partial(march_kernel, step_len), out_shape=(jax....]
where the time goes in v5:
time: 33.4 us; the launch traced here: 33.2 us
  Pallas kernels  31.8 us (95%)
  local copies, waits for them, and re-layouts  1.47 us (4%)
    pallas_call x1, Pallas kernels, composite(): pl.pallas_call(functools.partial(composite_head, bricks, tiles), out_shap...  19.4 us
    pallas_call x1, Pallas kernels, march(): pl.pallas_call(functools.partial(march_kernel, step_len), out_shape=(jax....  12.4 us
    unnamed x1, local copies, waits for them, and re-layouts  1.47 us

profile of v5, /device:TPU:1, one launch (start us, length us, event | category | flops | bytes accessed | tf_op | source)
XLA Modules:
  0.0 33.2 jit_solution(10221925646665403221)
XLA Ops:
  0.0 12.4 %march.1 = (f32[32,1024]{1,0:T(8,128)}, f32[1,1024]{1,0:T(1,128)}) custom-call(s32[1,1,1024]{2,1,0:T(1,128)} %entries_ref.1, s32[1,1,1024]{2,1,0:T(1,128)} %counts_ref.1, bf16[1,1,16,16384]{3,2,1,0:T(8,128)(2,1)} %bitcast.4, bf16[16,128]{1,0:T(8,128)(2,1)} %first_ref.1, bf16[33,128]{1,0:T(8,128)(2,1)} %bitcast.7), custom_call_target="tpu_custom_call" | custom-call | tf_op jit(solution)/shard_map/march/pallas_call | solution.py:106
  12.4 19.4 %composite_head.1 = bf16[16,16,128]{2,1,0:T(8,128)(2,1)} custom-call(s32[1,4]{1,0:T(1,128)} %rank_ref.1, f32[32,1024]{1,0:T(8,128)} %get-tuple-element.7.colour_ref, f32[1,1024]{1,0:T(1,128)} %get-tuple-element.8.depth_ref, bf16[9,32,128]{2,1,0:T(8,128)(2,1)} %conv_in_ref.1, bf16[3,384,128]{2,1,0:T(8,128)(2,1)} %bitcast.5, bf16[3,384,128]{2,1,0:T(8,128)(2,1)} %bitcast.6), custom_call_target="tpu_custom_call" | custom-call | tf_op jit(solution)/shard_map/composite_head/pallas_call | solution.py:322
  31.8 1.5 %copy.11 = bf16[16,16,128]{2,1,0:T(8,128)(2,1)} copy(bf16[16,16,128]{2,1,0:T(8,128)(2,1)} %composite_head.1) | data formatting | bytes 131072

commit v6 on v5

--- a/solution.py
+++ b/solution.py
@@ -61,7 +61,7 @@
         table[pl.ds(start, chunk), :] = jnp.transpose(joined)
         return carry
 
-    lax.fori_loop(0, cells // chunk, fill, 0, unroll=4)
+    lax.fori_loop(0, cells // chunk, fill, 0, unroll=8)
     pitch = windows.shape[0] // SAMPLES
     block_rays = pitch - 8
     slot = lax.broadcasted_iota(jnp.int32, (SAMPLES, lanes), 0)
@@ -232,14 +232,6 @@
     def _():
         side_copy(1).start()
 
-    @pl.when(tile > 0)
-    def _():
-        side_copy(0).wait_recv()
-
-    @pl.when(tile < tiles - 1)
-    def _():
-        side_copy(1).wait_recv()
-
     rows_in = ROWS_OWN + 2 * HALO
     half = COLS_DEV // 2
 
@@ -247,6 +239,15 @@
         return jnp.transpose(values.astype(jnp.float32)).reshape(rows_in, COLS_DEV, channels)
 
     own = pixels(strip[...])
+
+    @pl.when(tile > 0)
+    def _():
+        side_copy(0).wait_recv()
+
+    @pl.when(tile < tiles - 1)
+    def _():
+        side_copy(1).wait_recv()
+
     left = pixels(beside[0])
     right = pixels(beside[1])
     image = jnp.concatenate([left[:, half:], own, right[:, :half]], axis=1)

time: 33.4 us -> 32.7 us (0.979)
  Pallas kernels: 31.8 us -> 31 us
    pallas_call x1, Pallas kernels: 12.4 us -> 11.7 us  [march(): pl.pallas_call(functools.partial(march_kernel, step_len), out_shape=(jax....]
where the time goes in v6:
time: 32.7 us; the launch traced here: 32.5 us
  Pallas kernels  31 us (95%)
  local copies, waits for them, and re-layouts  1.47 us (4%)
    pallas_call x1, Pallas kernels, composite(): pl.pallas_call(functools.partial(composite_head, bricks, tiles), out_shap...  19.4 us
    pallas_call x1, Pallas kernels, march(): pl.pallas_call(functools.partial(march_kernel, step_len), out_shape=(jax....  11.7 us
    unnamed x1, local copies, waits for them, and re-layouts  1.47 us

profile of v6, /device:TPU:1, one launch (start us, length us, event | category | flops | bytes accessed | tf_op | source)
XLA Modules:
  0.0 32.5 jit_solution(15307942569233294063)
XLA Ops:
  0.0 11.7 %march.1 = (f32[32,1024]{1,0:T(8,128)}, f32[1,1024]{1,0:T(1,128)}) custom-call(s32[1,1,1024]{2,1,0:T(1,128)} %entries_ref.1, s32[1,1,1024]{2,1,0:T(1,128)} %counts_ref.1, bf16[1,1,16,16384]{3,2,1,0:T(8,128)(2,1)} %bitcast.4, bf16[16,128]{1,0:T(8,128)(2,1)} %first_ref.1, bf16[33,128]{1,0:T(8,128)(2,1)} %bitcast.7), custom_call_target="tpu_custom_call" | custom-call | tf_op jit(solution)/shard_map/march/pallas_call | solution.py:106
  11.7 19.4 %composite_head.1 = bf16[16,16,128]{2,1,0:T(8,128)(2,1)} custom-call(s32[1,4]{1,0:T(1,128)} %rank_ref.1, f32[32,1024]{1,0:T(8,128)} %get-tuple-element.7.colour_ref, f32[1,1024]{1,0:T(1,128)} %get-tuple-element.8.depth_ref, bf16[9,32,128]{2,1,0:T(8,128)(2,1)} %conv_in_ref.1, bf16[3,384,128]{2,1,0:T(8,128)(2,1)} %bitcast.5, bf16[3,384,128]{2,1,0:T(8,128)(2,1)} %bitcast.6), custom_call_target="tpu_custom_call" | custom-call | tf_op jit(solution)/shard_map/composite_head/pallas_call | solution.py:323
  31.0 1.5 %copy.11 = bf16[16,16,128]{2,1,0:T(8,128)(2,1)} copy(bf16[16,16,128]{2,1,0:T(8,128)(2,1)} %composite_head.1) | data formatting | bytes 131072

commit v7 on v6

--- a/solution.py
+++ b/solution.py
@@ -297,7 +297,7 @@
     second = jnp.where(inside(-1, count), jnp.maximum(second, 0.0), 0.0)
     frame = convolve(second, conv_out_ref, ROWS_OWN)
     frame = frame.reshape(ROWS_OWN, WIDE, frame.shape[1])[:, half : half + COLS_DEV]
-    frame_ref[...] = frame.astype(jnp.bfloat16)
+    frame_ref[...] = frame
 
     for peer in peers:
         depth_copy(peer, me).wait_send()
@@ -322,7 +322,7 @@
     dma = pltpu.SemaphoreType.DMA
     return pl.pallas_call(
         functools.partial(composite_head, bricks, tiles),
-        out_shape=jax.ShapeDtypeStruct((ROWS_OWN, COLS_DEV, outs), jnp.bfloat16),
+        out_shape=jax.ShapeDtypeStruct((ROWS_OWN, COLS_DEV, outs), jnp.float32),
         in_specs=[pl.BlockSpec(memory_space=pltpu.SMEM)] + [vmem] * 5,
         out_specs=vmem,
         scratch_shapes=[
@@ -366,7 +366,8 @@
     colour, depth_sum = march(
         entry_cells, sample_counts, brick_features, input_layer_weight, second_weight
     )
-    return composite(brick_rank, colour, depth_sum, conv_in, conv_mid, conv_out)
+    frame = composite(brick_rank, colour, depth_sum, conv_in, conv_mid, conv_out)
+    return frame.astype(jnp.bfloat16)
 
 
 def solution(mesh):

time: 32.7 us -> 32.8 us (level)
  other arithmetic: 0 us -> 1.54 us
  local copies, waits for them, and re-layouts: 1.47 us -> 0 us
    convert_element_type x0 -> x1, other arithmetic: none -> 1.54 us  [shards(): return frame.astype(jnp.bfloat16)]
    unnamed x1 -> x0, local copies, waits for them, and re-layouts: 1.47 us -> none
where the time goes in v7:
time: 32.8 us; the launch traced here: 32.6 us
  Pallas kernels  31 us (95%)
  other arithmetic  1.54 us (5%)
    pallas_call x1, Pallas kernels, composite(): pl.pallas_call(functools.partial(composite_head, bricks, tiles), out_shap...  19.4 us
    pallas_call x1, Pallas kernels, march(): pl.pallas_call(functools.partial(march_kernel, step_len), out_shape=(jax....  11.7 us
    convert_element_type x1, other arithmetic, shards(): return frame.astype(jnp.bfloat16)  1.54 us

profile of v7, /device:TPU:1, one launch (start us, length us, event | category | flops | bytes accessed | tf_op | source)
XLA Modules:
  0.0 32.6 jit_solution(16914165611098756248)
XLA Ops:
  0.0 11.7 %march.1 = (f32[32,1024]{1,0:T(8,128)}, f32[1,1024]{1,0:T(1,128)}) custom-call(s32[1,1,1024]{2,1,0:T(1,128)} %entries_ref.1, s32[1,1,1024]{2,1,0:T(1,128)} %counts_ref.1, bf16[1,1,16,16384]{3,2,1,0:T(8,128)(2,1)} %bitcast.4, bf16[16,128]{1,0:T(8,128)(2,1)} %first_ref.1, bf16[33,128]{1,0:T(8,128)(2,1)} %bitcast.7), custom_call_target="tpu_custom_call" | custom-call | tf_op jit(solution)/shard_map/march/pallas_call | solution.py:106
  11.7 19.4 %composite_head.1 = f32[16,16,128]{2,1,0:T(8,128)} custom-call(s32[1,4]{1,0:T(1,128)} %rank_ref.1, f32[32,1024]{1,0:T(8,128)} %get-tuple-element.7.colour_ref, f32[1,1024]{1,0:T(1,128)} %get-tuple-element.8.depth_ref, bf16[9,32,128]{2,1,0:T(8,128)(2,1)} %conv_in_ref.1, bf16[3,384,128]{2,1,0:T(8,128)(2,1)} %bitcast.5, bf16[3,384,128]{2,1,0:T(8,128)(2,1)} %bitcast.6), custom_call_target="tpu_custom_call" | custom-call | tf_op jit(solution)/shard_map/composite_head/pallas_call | solution.py:323
  31.1 1.5 %convert_element_type.3 = bf16[16,16,128]{2,1,0:T(8,128)(2,1)} convert(f32[16,16,128]{2,1,0:T(8,128)} %composite_head.1) | non-fusion elementwise | flops 32768 | bytes 196608 | tf_op jit(solution)/shard_map/convert_element_type | solution.py:370
